TPU v7x, 256 devices: a whole 4x4x8 slice. The times are simulated.
256 devices in a mesh: chan: 32 (over x, z), rows: 8 (over y, core).
Axes of the slice: x: 4, y: 4, z: 8, core: 2. Of those that a mesh axis runs over, the one named last changes fastest.
Arguments:
- row_cells: int32 [256, 2048], P('chan', 'rows'), may hold values from 0 to 127
- col_cells: int32 [256, 2048], P('chan', 'rows'), may hold values from 0 to 2047
- visibilities: float32 [256, 2, 2048], P('chan', None, 'rows'), may hold values from -6 to 6
- imaging_weights: float32 [256, 2048], P('chan', 'rows'), may hold values from 0.05 to 1
- taylor_weights: float32 [256, 3], P('chan'), may hold values from -4 to 4
- kernel_taps: float32 [8], replicated, may hold values from 0.1 to 1
Outputs:
- normalized_grids: float32 [2048, 3, 2, 1024], P('chan', None, None, 'rows')
Inputs may be any that keep to these rules, and one draw needn't show every extreme that they name: `row_cells`: a visibility's centre row within its slab.
All inputs are finite; a program needn't handle non-finite values.
Results may differ from a plain program's by a relative error of at most 0.0041.
Values sent between devices are 32-bit elements; how exact they have to be, the bound alone decides.
A program may use at most 384 MiB of HBM per device.

v0:
```python
import jax
import jax.numpy as jnp
from jax import lax
from jax.sharding import PartitionSpec as P

NCOL = 2048
TERMS = 3
ROWS_DEV = 128


def invert_three(matrix):
    first_row = matrix[0]
    second_row = matrix[1]
    third_row = matrix[2]
    across = jnp.stack(
        [
            jnp.cross(second_row, third_row),
            jnp.cross(third_row, first_row),
            jnp.cross(first_row, second_row),
        ],
        axis=1,
    )
    determinant = jnp.sum(first_row * across[:, 0])
    return across / determinant


def lookup(offset, kernel):
    summed = jnp.zeros(offset.shape, jnp.float32)
    for tap_number in range(kernel.shape[0]):
        summed = summed + jnp.where(offset == tap_number, kernel[tap_number], jnp.float32(0.0))
    return summed


def row_kernel(vis_piece, weight_piece, taylor_piece, row_piece, kernel, slab_rows):
    centre = kernel.shape[0] // 2
    scaled = taylor_piece[:, :, None, None] * (
        weight_piece[:, None, None, :] * vis_piece[:, None, :, :]
    )
    offset = jnp.arange(slab_rows, dtype=jnp.int32)[None, None, :] - row_piece[:, :, None] + centre
    row_taps = lookup(offset, kernel)
    weighted = jnp.transpose(scaled, (0, 3, 1, 2))[..., None] * row_taps[:, :, None, None, :]
    how_many = row_piece.shape[0] * row_piece.shape[1]
    return weighted.astype(jnp.bfloat16).reshape(how_many, -1)


def col_kernel(col_piece, width_now, taps_round):
    centre = taps_round.shape[0] // 2
    columns = jnp.arange(width_now, dtype=jnp.int32)
    offset = columns[None, :] - col_piece.reshape(-1)[:, None] + centre
    return lookup(offset, taps_round).astype(jnp.bfloat16)


def grid_part(col_taps, row_taps, width_now, slab_rows):
    product = lax.dot_general(
        col_taps, row_taps, (((0,), (0,)), ((), ())), preferred_element_type=jnp.float32
    )
    return product.reshape(width_now, TERMS, 2, slab_rows)


def hessian_part(taylor_piece, weight_piece):
    chan_sum = jnp.sum(weight_piece, axis=1)
    return jnp.einsum(
        "ca,cb,c->ab", taylor_piece, taylor_piece, chan_sum, precision=lax.Precision.HIGHEST
    )


def body(row_cells, col_cells, visibilities, imaging_weights, taylor_weights, kernel_taps):
    taps_round = kernel_taps.astype(jnp.bfloat16).astype(jnp.float32)
    cols_dev = NCOL // lax.axis_size("chan")
    row_taps = row_kernel(
        visibilities, imaging_weights, taylor_weights, row_cells, kernel_taps, ROWS_DEV
    )
    col_taps = col_kernel(col_cells, cols_dev * lax.axis_size("chan"), taps_round)
    taylor_grid = lax.psum_scatter(
        grid_part(col_taps, row_taps, cols_dev * lax.axis_size("chan"), ROWS_DEV),
        "chan",
        scatter_dimension=0,
        tiled=True,
    )
    hessian = lax.psum(hessian_part(taylor_weights, imaging_weights), ("chan", "rows"))
    inverse = invert_three(hessian / hessian[0, 0])
    return jnp.einsum("ab,cbir->cair", inverse, taylor_grid, precision=lax.Precision.HIGHEST)


def solution(mesh):
    in_specs = (
        P("chan", "rows"),
        P("chan", "rows"),
        P("chan", None, "rows"),
        P("chan", "rows"),
        P("chan", None),
        P(),
    )
    out_specs = P("chan", None, None, "rows")
    return jax.shard_map(body, mesh=mesh, in_specs=in_specs, out_specs=out_specs, check_vma=False)
```

profile of v0, /device:TPU:1, one launch (start us, length us, event | category | flops | bytes accessed | tf_op | source)
XLA Modules:
  0.0 269.1 jit_solution(3623702759064454623)
XLA Ops:
  6.5 0.0 copy-start.2
  6.5 0.0 all-reduce.3.cloned.1.call-start
  6.5 1.6 fusion.56
  8.2 0.7 convert_convert_fusion
  8.8 0.7 multiply_bitcast_fusion
  9.6 0.8 broadcast_multiply_fusion
  10.3 6.5 %select_add_fusion = f32[8,256,128]{1,0,2:T(8,128)S(1)} fusion(f32[]{:T(128)} %bitcast.18, f32[]{:T(128)} %bitcast.17, f32[]{:T(128)} %bitcast.16, f32[]{:T(128)} %bitcast.15, f32[]{:T(128)} %bitcast.14, f32[]{:T(128)} %bitcast.13, f32[]{:T(128)} %bitcast.12, f32[]{:T(128)} %bitcast.11, s32[8,256]{1,0:T(8,128)} %param.8), kind=kLoop, calls=%fused_computation.33 | loop fusion | flops 6553600 | bytes 1056800 | tf_op jit(solution)/shard_map/add | solution.py:30
  16.8 0.7 multiply_convert_fusion
  17.5 1.1 copy.29
  18.5 0.7 fusion.55
  19.2 0.0 copy-done.2
  19.2 25.4 %fusion.9 = f32[2048,3,2,128]{3,0,2,1:T(8,128)S(1)} fusion(bf16[3,2,128,2048]{3,2,1,0:T(8,128)(2,1)S(1)} %bitcast.53, f32[]{:T(128)} %bitcast.7, f32[]{:T(128)} %bitcast.6, f32[]{:T(128)} %bitcast.5, f32[]{:T(128)} %bitcast.4, f32[]{:T(128)} %bitcast.3, f32[]{:T(128)} %bitcast.2, f32[]{:T(128)} %bitcast.1, f32[]{:T(128)} %bitcast, s32[2048]{0:T(1024)S(1)} %bitcast.55), kind=kOutput, calls=%fused_computation.11 | convolution fusion | flops 6551502848 | bytes 9445408 | tf_op jit(solution)/shard_map/dot_general | solution.py:54
  44.7 25.7 %copy.20 = f32[2048,3,2,128]{3,2,1,0:T(2,128)} copy(f32[2048,3,2,128]{3,0,2,1:T(8,128)S(1)} %fusion.9) | data formatting | bytes 12582912 | tf_op jit(solution)/shard_map/dot_general | solution.py:54
  70.3 0.0 copy-start
  70.3 0.0 copy-start.1
  70.3 0.0 copy-start.3
  70.3 0.0 all-reduce.3.cloned.1.call-update
  70.3 0.7 copy-done
  71.0 0.1 reduce_sum.18
  71.1 0.0 copy-done.1
  71.1 0.1 convolution_bitcast_fusion.1
  71.3 83.9 %psum.7 = f32[3,3]{0,1:T(4,128)S(1)} all-reduce(f32[3,3]{0,1:T(4,128)S(1)} %convolution_bitcast_fusion.1), channel_id=1, replica_groups=mesh['chan'=32,'rows'=8] {'chan','rows'}, use_global_device_ids=true, to_apply=%region_2.3 | all-reduce | flops 9 | bytes 72 | tf_op jit(solution)/shard_map/psum | solution.py:80
  155.2 0.5 slice.94
  155.7 0.6 broadcast_divide_fusion
  156.3 0.2 slice_reduce_fusion.1
  156.6 0.7 fusion.54
  157.2 0.7 fusion.52
  180.7 0.1 maximum_bitcast_fusion.1
  180.8 0.1 copy.23
  180.9 0.1 maximum_bitcast_fusion
  181.0 0.1 copy.22
  181.1 0.7 multiply_reduce_fusion
  181.8 0.1 copy.21
  181.9 0.0 copy-done.3
  181.9 0.6 dynamic-slice
  183.1 76.2 %all-reduce.3.cloned.1.call-done = f32[2048,3,2,128]{3,2,1,0:T(2,128)} async-done(((f32[2048,3,2,128]{3,2,1,0:T(2,128)}), f32[2048,3,2,128]{3,2,1,0:T(2,128)}) %all-reduce.3.cloned.1.call-update) | async-done | bytes 6291472
  259.3 1.0 constant_dynamic-slice_fusion
  260.2 1.2 convolution_bitcast_fusion
  261.5 0.8 copy.25
  (2 shorter events, 0.0 us)
Async XLA Ops:
  6.5 12.7 %copy-start.2 = (s32[8,256]{1,0:T(8,128)S(1)}, s32[8,256]{1,0:T(8,128)}, u32[]{:S(2)}) copy-start(s32[8,256]{1,0:T(8,128)} %param.9) | copy-start | bytes 24580
  6.5 252.7 %all-reduce.3.cloned.1.call-start = ((), (), s32[]{:S(2)}) async-start(), calls=%async_computation | async-start | bytes 12582912
  70.3 0.7 copy-start
  70.3 0.8 copy-start.1
  70.3 111.6 %copy-start.3 = (u32[256]{0:T(256)S(1)}, u32[256]{0:T(256)}, u32[]{:S(2)}) copy-start(u32[256]{0:T(256)} %constant.8) | copy-start | bytes 3076
Sparse Core Ops, SparseCore 0:
  70.5 188.7 all-reduce.2
where the time goes:
time: 270 us; the launch traced here: 269 us
  blocking collectives  83.9 us (31%)
  waiting for transfers between devices  76.2 us (28%)
  between operations  37 us (14%)
  local copies, waits for them, and re-layouts  34.4 us (13%)
  matrix products  26.8 us (10%)
  other arithmetic  10.9 us (4%)
    psum x1, blocking collectives, body(): lax.psum(hessian_part(taylor_weights, imaging_weights), ('chan', 'rows'))  83.9 us
    unnamed x2, waiting for transfers between devices  76.2 us
    dot_general x1, local copies, waits for them, and re-layouts, grid_part(): lax.dot_general(col_taps, row_taps, (((0,), (0,)), ((), ())), preferred_e...  25.7 us
    dot_general x1, matrix products, grid_part(): lax.dot_general(col_taps, row_taps, (((0,), (0,)), ((), ())), preferred_e...  25.4 us
    add x1, other arithmetic, lookup(): summed + jnp.where(offset == tap_number, kernel[tap_number], jnp.float32(...  6.48 us
  transfers between devices with their start and end apart: 1, of which 1 were waited for; matrix products, arithmetic and copies ran while one was open for 2% of the time, Pallas kernels for 0%

commit v1 on v0

v1 whole, which is shorter than its diff:
```python
import functools

import jax
import jax.numpy as jnp
from jax import lax
from jax.experimental import pallas as pl
from jax.experimental.pallas import tpu as pltpu
from jax.sharding import PartitionSpec as P

NCOL = 2048
TERMS = 3
ROWS_DEV = 128
SUPPORT = 8
CENTRE = SUPPORT // 2
SLOTS = 128
PAIRS = ((0, 0), (0, 1), (0, 2), (1, 1), (1, 2), (2, 2))
ACROSS_X, ACROSS_Z = 4, 8
HALF = 48
PER_STEP = 4

MESH = pl.DeviceIdType.MESH
F32 = jnp.float32
BF16 = jnp.bfloat16


def ring_distance(step, length):
    return min(step % length, -step % length)


def near_first():
    steps = [(x, z) for x in range(ACROSS_X) for z in range(ACROSS_Z)]
    return sorted(steps, key=lambda s: (ring_distance(s[0], ACROSS_X) + ring_distance(s[1], ACROSS_Z), s))


def matmul_nt(a, b):
    return lax.dot_general(a, b, (((1,), (1,)), ((), ())), preferred_element_type=F32)


def matmul(a, b):
    return lax.dot_general(a, b, (((1,), (0,)), ((), ())), preferred_element_type=F32)


def iota(shape, axis):
    return lax.broadcasted_iota(jnp.int32, shape, axis)


def two_parts(value):
    high = value.astype(BF16)
    return high, (value - high.astype(F32)).astype(BF16)


def kernel(
    chans, n_rows, width,
    round_ref, row_ref, col_ref, vis_ref, weight_ref, taylor_ref, taps_ref,
    out_ref, rounds_ref,
    mine, theirs, a_ref, b_ref, e_ref, cells, mixed, hess_mine, hess_rows, hess_sum, hess_chan,
    send_sem, recv_sem, row_send, row_recv, hess_send, hess_recv,
):
    me, slab = lax.axis_index("chan"), lax.axis_index("rows")
    my_x, my_z = me // ACROSS_Z, me % ACROSS_Z
    steps = near_first()
    half = chans // 2
    n_chan = row_ref.shape[0]
    pieces = [(c, h) for c in range(n_chan) for h in range(2)]

    def partner(step):
        return ((my_x + step[0]) % ACROSS_X) * ACROSS_Z + (my_z + step[1]) % ACROSS_Z

    def place(owner):
        return (owner % 2) * half + owner // 2

    barrier = pltpu.get_barrier_semaphore()
    for step in steps[:0:-1]:
        pl.semaphore_signal(barrier, inc=1, device_id=(partner(step), slab), device_id_type=MESH)
    for i in range(1, n_rows):
        pl.semaphore_signal(barrier, inc=1, device_id=(me, (slab + i) % n_rows), device_id_type=MESH)

    col = col_ref[...].astype(F32)
    owner = iota((2 * half, 128), 0)
    owner = jnp.where(owner < half, 2 * owner, 2 * (owner - half) + 1)
    first = (owner * width - (SUPPORT - 1 - CENTRE)).astype(F32)
    reach = []
    for n, (c, h) in enumerate(pieces):
        at = col[c : c + 1, h * 128 : h * 128 + 128] - first
        inside = (at >= 0.0) & (at <= float(width + SUPPORT - 2))
        hit = jnp.where(inside, 1.0, 0.0)
        reach.append(hit)
        e_ref[n * 2 * half : (n + 1) * 2 * half, :] = hit.astype(BF16)
        at = jnp.where(inside, at, 0.0).astype(BF16)
        for par in range(2):
            a_ref[par, 13 * half : 14 * half, n * 128 : n * 128 + 128] = at[par * half : (par + 1) * half]
    before = jnp.where(iota((128, 256), 0) < iota((128, 256), 1), 1.0, 0.0).astype(BF16)
    counts = matmul(e_ref[...], before)
    start = jnp.zeros((2 * half, 128), F32)
    base = (round_ref[0] * SLOTS).astype(F32)
    slot = iota((SLOTS, 128), 0).astype(F32)
    for n in range(len(pieces)):
        now = counts[n * 2 * half : (n + 1) * 2 * half]
        rank = reach[n] * (now[:, :128] + start)
        start = start + now[:, 128:]
        for par in range(2):
            which = jnp.sum(rank[par * half : (par + 1) * half], axis=0, keepdims=True) - base
            b_ref[par, :, n * 128 : n * 128 + 128] = jnp.where(slot == which, 1.0, 0.0).astype(BF16)
    fullest = jnp.max(start, axis=0, keepdims=True)

    weight = weight_ref[...]
    taylor = taylor_ref[...]
    chan_sum = jnp.sum(weight, axis=1, keepdims=True)
    lane = iota((1, 128), 1)
    part = jnp.where(lane == len(PAIRS), fullest, 0.0)
    for i, (a, b) in enumerate(PAIRS):
        entry = jnp.sum(taylor[:, a : a + 1] * taylor[:, b : b + 1] * chan_sum, axis=0, keepdims=True)
        part = part + jnp.where(lane == i, entry, 0.0)

    def gather(values):
        return jnp.where(lane == len(PAIRS), jnp.max(values, axis=0), jnp.sum(values, axis=0))

    hess_mine[...] = part
    hess_rows[pl.ds(slab, 1)] = part[None]

    scaled = []
    for t in range(TERMS):
        for p in range(2):
            scaled.append(taylor[:, t : t + 1] * (weight * vis_ref[:, p, :]))
    rows = [two_parts(value) for value in scaled]
    rows = [high for high, _ in rows] + [low for _, low in rows] + [row_ref[...].astype(F32).astype(BF16)]
    rows = [value.astype(F32) for value in rows]
    for n, (c, h) in enumerate(pieces):
        hit = reach[n].astype(BF16)
        for i, value in enumerate(rows):
            spread = jnp.broadcast_to(value[c : c + 1, h * 128 : h * 128 + 128], (half, 128)).astype(BF16)
            for par in range(2):
                a_ref[par, i * half : (i + 1) * half, n * 128 : n * 128 + 128] = (
                    hit[par * half : (par + 1) * half] * spread
                )
    for par in range(2):
        tile = matmul_nt(a_ref[par], b_ref[par])
        for i in range(8):
            if i < 6:
                value = tile[i * half : (i + 1) * half] + tile[(6 + i) * half : (7 + i) * half]
            else:
                value = tile[(6 + i) * half : (7 + i) * half]
            mine[pl.ds(par * half * 8 + i, half, stride=8), :] = value

    pl.semaphore_wait(barrier, chans - 1 + n_rows - 1)
    row_copies = []
    for i in range(1, n_rows):
        to = (slab + i) % n_rows
        copy = pltpu.make_async_remote_copy(
            src_ref=hess_mine, dst_ref=hess_rows.at[slab], send_sem=row_send.at[i], recv_sem=row_recv.at[i],
            device_id=(me, to), device_id_type=MESH,
        )
        copy.start()
        row_copies.append(copy)
    copies = {}
    for step in steps[:0:-1]:
        to = partner(step)
        i = steps.index(step)
        copy = pltpu.make_async_remote_copy(
            src_ref=mine.at[pl.ds(pl.multiple_of(place(to) * 8, 8), 8)], dst_ref=theirs.at[i],
            send_sem=send_sem.at[i], recv_sem=recv_sem.at[i],
            device_id=(to, slab), device_id_type=MESH,
        )
        copy.start()
        copies[i] = copy
    theirs[0] = mine[pl.ds(pl.multiple_of(place(me) * 8, 8), 8), :]
    for copy in row_copies:
        copy.wait_recv()
    row_sum = gather(hess_rows[...])
    hess_sum[...] = row_sum
    hess_chan[0] = row_sum
    hess_copies = []
    for i in range(len(steps) - 1, 0, -1):
        copy = pltpu.make_async_remote_copy(
            src_ref=hess_sum, dst_ref=hess_chan.at[i], send_sem=hess_send.at[i], recv_sem=hess_recv.at[i],
            device_id=(partner(steps[i]), slab), device_id_type=MESH,
        )
        copy.start()
        hess_copies.append(copy)

    tap_of = iota((ROWS_DEV, ROWS_DEV), 1) - iota((ROWS_DEV, ROWS_DEV), 0) + CENTRE
    row_taps = jnp.zeros((ROWS_DEV, ROWS_DEV), F32)
    for k in range(SUPPORT):
        row_taps = jnp.where(tap_of == k, taps_ref[k], row_taps)
    row_high, row_low = two_parts(row_taps)

    half_cell = iota((HALF, 128), 0).astype(F32)
    row_cell = iota((2 * ROWS_DEV, 128), 0).astype(F32)
    for g in range(0, len(steps), PER_STEP):
        a_parts, b_parts = [], []
        for i in range(g, g + PER_STEP):
            if i > 0:
                copies[i].wait_recv()
            tile = theirs[i]
            high = tile.astype(BF16).astype(F32)
            low = tile - high
            at = tile[7:8]
            halves = jnp.floor(at * 0.5)
            key = tile[6:7] + (at - 2.0 * halves) * float(ROWS_DEV)
            b_parts.append(jnp.where(row_cell == key, 1.0, 0.0).astype(BF16))
            here = half_cell == halves
            a_parts.append(
                jnp.concatenate(
                    [jnp.where(here, part_of[v : v + 1], 0.0).astype(BF16) for part_of in (high, low) for v in range(6)],
                    axis=0,
                )
            )
        total = matmul_nt(jnp.concatenate(a_parts, axis=1), jnp.concatenate(b_parts, axis=1))
        if g == 0:
            cells[...] = total
        else:
            cells[...] += total

    for par in range(2):
        x = cells[: 6 * HALF, par * 128 : par * 128 + 128] + cells[6 * HALF :, par * 128 : par * 128 + 128]
        high, low = two_parts(x)
        mixed[par * 6 * HALF : (par + 1) * 6 * HALF, :] = (
            matmul(high, row_high) + matmul(low, row_high) + matmul(high, row_low)
        )

    for copy in hess_copies:
        copy.wait_recv()
    hess = gather(hess_chan[...])
    entries = {}
    for i, (a, b) in enumerate(PAIRS):
        entries[a, b] = entries[b, a] = jnp.sum(jnp.where(lane == i, hess, 0.0), axis=1, keepdims=True)
    scale = entries[0, 0]
    m = [[entries[a, b] / scale for b in range(3)] for a in range(3)]

    def cross(u, v):
        return [u[1] * v[2] - u[2] * v[1], u[2] * v[0] - u[0] * v[2], u[0] * v[1] - u[1] * v[0]]

    across = [cross(m[1], m[2]), cross(m[2], m[0]), cross(m[0], m[1])]
    det = m[0][0] * across[0][0] + m[0][1] * across[0][1] + m[0][2] * across[0][2]
    inverse = [[across[b][a] / det for b in range(3)] for a in range(3)]
    count = jnp.max(jnp.where(lane == len(PAIRS), hess, 0.0))
    rounds_ref[0] = (count.astype(jnp.int32) + (SLOTS - 1)) // SLOTS

    wide = width // 2
    col_taps = [jnp.full((8, 128), taps_ref[j], F32).astype(BF16).astype(F32)[:1] for j in range(SUPPORT)]
    for e in range(2):
        for p in range(2):
            grids = []
            for t in range(TERMS):
                grid = jnp.zeros((wide, 128), F32)
                for j in range(SUPPORT):
                    shift = e + SUPPORT - 1 - j
                    at = ((shift % 2) * 6 + t * 2 + p) * HALF + shift // 2
                    grid = grid + col_taps[j] * mixed[at : at + wide, :]
                grids.append(grid)
            for a in range(TERMS):
                value = inverse[a][0] * grids[0] + inverse[a][1] * grids[1] + inverse[a][2] * grids[2]
                out_ref[pl.ds(e * 6 + a * 2 + p, wide, stride=12), :] = value

    for copy in row_copies + hess_copies + list(copies.values()):
        copy.wait_send()


def grid_round(chans, n_rows, width, which, arrays):
    vmem, smem = pl.BlockSpec(memory_space=pltpu.VMEM), pl.BlockSpec(memory_space=pltpu.SMEM)
    n_vis = arrays[0].shape[0] * arrays[0].shape[1]
    return pl.pallas_call(
        functools.partial(kernel, chans, n_rows, width),
        out_shape=(
            jax.ShapeDtypeStruct((width * TERMS * 2, ROWS_DEV), F32),
            jax.ShapeDtypeStruct((1,), jnp.int32),
        ),
        in_specs=[smem] + [vmem] * 5 + [smem],
        out_specs=(vmem, smem),
        scratch_shapes=[
            pltpu.VMEM((chans * 8, SLOTS), F32),
            pltpu.VMEM((chans, 8, SLOTS), F32),
            pltpu.VMEM((2, 14 * chans // 2, n_vis), BF16),
            pltpu.VMEM((2, SLOTS, n_vis), BF16),
            pltpu.VMEM((n_vis // 128 * chans, 128), BF16),
            pltpu.VMEM((12 * HALF, 2 * ROWS_DEV), F32),
            pltpu.VMEM((12 * HALF, ROWS_DEV), F32),
            pltpu.VMEM((1, 128), F32),
            pltpu.VMEM((n_rows, 1, 128), F32),
            pltpu.VMEM((1, 128), F32),
            pltpu.VMEM((chans, 1, 128), F32),
            pltpu.SemaphoreType.DMA((chans,)),
            pltpu.SemaphoreType.DMA((chans,)),
            pltpu.SemaphoreType.DMA((n_rows,)),
            pltpu.SemaphoreType.DMA((n_rows,)),
            pltpu.SemaphoreType.DMA((chans,)),
            pltpu.SemaphoreType.DMA((chans,)),
        ],
        compiler_params=pltpu.CompilerParams(
            collective_id=0, has_side_effects=True, vmem_limit_bytes=40 * 1024 * 1024
        ),
    )(which, *arrays)


def body(*arrays):
    chans, n_rows = lax.axis_size("chan"), lax.axis_size("rows")
    width = NCOL // chans

    def more(state):
        return state[0] < state[1]

    def step(state):
        done, _, total = state
        part, rounds = grid_round(chans, n_rows, width, done[None], arrays)
        return done + 1, rounds[0], total + part

    part, rounds = grid_round(chans, n_rows, width, jnp.zeros((1,), jnp.int32), arrays)
    _, _, total = lax.while_loop(more, step, (jnp.int32(1), rounds[0], part))
    return total.reshape(width, TERMS, 2, ROWS_DEV)


def solution(mesh):
    in_specs = (
        P("chan", "rows"),
        P("chan", "rows"),
        P("chan", None, "rows"),
        P("chan", "rows"),
        P("chan", None),
        P(),
    )
    out_specs = P("chan", None, None, "rows")
    return jax.shard_map(body, mesh=mesh, in_specs=in_specs, out_specs=out_specs, check_vma=False)
```

time: 270 us -> 24.9 us (0.09)
  blocking collectives: 83.9 us -> 0 us
  waiting for transfers between devices: 76.2 us -> 0 us
  between operations: 37 us -> 0.06 us
  local copies, waits for them, and re-layouts: 34.4 us -> 1.47 us
  matrix products: 26.8 us -> 0 us
  Pallas kernels: 0 us -> 22.5 us
  other arithmetic: 10.9 us -> 0 us
    psum x1 -> x0, blocking collectives: 83.9 us -> none  [body(): lax.psum(hessian_part(taylor_weights, imaging_weights), ('chan', 'rows'))]
    unnamed x2 -> x0, waiting for transfers between devices: 76.2 us -> none
    dot_general x3 -> x0, matrix products: 26.8 us -> none  [the longest x1 25.4 us: grid_part(): lax.dot_general(col_taps, row_taps, (((0,), (0,)), ((), ())), preferred_e...]
    dot_general x1 -> x0, local copies, waits for them, and re-layouts: 25.7 us -> none  [grid_part(): lax.dot_general(col_taps, row_taps, (((0,), (0,)), ((), ())), preferred_e...]
    pallas_call x0 -> x1, Pallas kernels: none -> 22.5 us  [grid_round(): pl.pallas_call(functools.partial(kernel, chans, n_rows, width), out_shape...]
    add x1 -> x0, other arithmetic: 6.48 us -> none  [lookup(): summed + jnp.where(offset == tap_number, kernel[tap_number], jnp.float32(...]
    slice x6 -> x0, local copies, waits for them, and re-layouts: 4.34 us -> none  [the longest x2 2.28 us: lookup(): kernel[tap_number]]
  transfers between devices with their start and end apart: 1 -> 0, of which waited for: 1 -> 0; matrix products, arithmetic and copies ran while one was open for 2% -> 0% of each run, Pallas kernels for 0% -> 0%
where the time goes in v1:
time: 24.9 us; the launch traced here: 24.7 us
  Pallas kernels  22.5 us (90%)
  local copies, waits for them, and re-layouts  1.47 us (6%)
  loops' own time  0.69 us (3%)
    pallas_call x1, Pallas kernels, grid_round(): pl.pallas_call(functools.partial(kernel, chans, n_rows, width), out_shape...  22.5 us
    unnamed x12, local copies, waits for them, and re-layouts  1.47 us
    another operation x1, loops' own time, body(): _, _, total = lax.while_loop(more, step, (jnp.int32(1), rounds[0], part))  0.69 us

profile of v1, /device:TPU:1, one launch (start us, length us, event | category | flops | bytes accessed | tf_op | source)
XLA Modules:
  0.0 24.7 jit_solution(16677155626835404333)
XLA Ops:
  0.0 0.0 copy-start.4
  0.0 0.8 %copy.7.taylor_ref = f32[8,3]{1,0:T(8,128)S(1)} copy(f32[8,3]{0,1:T(4,128)} %param.12) | data formatting | bytes 192 | tf_op args[4]
  0.8 0.0 copy-done.4
  0.8 0.0 copy-start
  0.8 0.0 copy-start.1
  0.8 0.0 copy-start.2
  0.8 0.0 copy-start.3
  0.8 22.5 %shard_map.64 = (f32[384,128]{1,0:T(8,128)S(1)}, s32[1]{0:T(128)}) custom-call(s32[1]{0:T(128)} %constant.2.clone.1.round_ref, s32[8,256]{1,0:T(8,128)} %row_ref.1, s32[8,256]{1,0:T(8,128)} %col_ref.1, f32[8,2,256]{2,1,0:T(2,128)} %vis_ref.1, f32[8,256]{1,0:T(8,128)} %weight_ref.1, f32[8,3]{1,0:T(8,128)S(1)} %copy.7.taylor_ref, f32[8]{0:T(128)S(1)} %copy-done.4), custom_call_target="tpu_custom_call" | custom-call | tf_op jit(solution)/shard_map/pallas_call | solution.py:262
  23.3 0.0 copy-done
  23.3 0.0 copy-done.1
  23.3 0.0 copy-done.2
  23.3 0.0 copy-done.3
  23.3 0.7 %while.12 = (s32[]{:T(128)}, s32[]{:T(128)}, f32[384,128]{1,0:T(8,128)S(1)}, s32[8,256]{1,0:T(8,128)S(1)}, s32[8,256]{1,0:T(8,128)S(1)}, /*index=5*/f32[8,2,256]...) while((s32[]{:T(128)}, s32[]{:T(128)}, f32[384,128]{1,0:T(8,128)S(1)}, ...), condition=%wide.region_1.0_spmd, body=%wide.region_0.0_spmd.sunk | while | flops 49154 | bytes 589933 | solution.py:308
  24.0 0.7 %copy.19 = f32[64,3,2,128]{3,2,1,0:T(2,128)} copy(f32[64,3,2,128]{3,2,1,0:T(2,128)S(1)} %bitcast.8) | data formatting | bytes 393216
Async XLA Ops:
  0.0 0.8 %copy-start.4 = (f32[8]{0:T(128)S(1)}, f32[8]{0:T(128)}, u32[]{:S(2)}) copy-start(f32[8]{0:T(128)} %taps_ref.1) | copy-start | bytes 100
  0.8 22.5 %copy-start = (f32[8,2,256]{2,1,0:T(2,128)S(1)}, f32[8,2,256]{2,1,0:T(2,128)}, u32[]{:S(2)}) copy-start(f32[8,2,256]{2,1,0:T(2,128)} %vis_ref.1) | copy-start | bytes 49156
  0.8 22.5 %copy-start.1 = (s32[8,256]{1,0:T(8,128)S(1)}, s32[8,256]{1,0:T(8,128)}, u32[]{:S(2)}) copy-start(s32[8,256]{1,0:T(8,128)} %row_ref.1) | copy-start | bytes 24580
  0.8 22.5 %copy-start.2 = (s32[8,256]{1,0:T(8,128)S(1)}, s32[8,256]{1,0:T(8,128)}, u32[]{:S(2)}) copy-start(s32[8,256]{1,0:T(8,128)} %col_ref.1) | copy-start | bytes 24580
  0.8 22.5 %copy-start.3 = (f32[8,256]{1,0:T(8,128)S(1)}, f32[8,256]{1,0:T(8,128)}, u32[]{:S(2)}) copy-start(f32[8,256]{1,0:T(8,128)} %weight_ref.1) | copy-start | bytes 24580

commit v2 on v1

--- a/solution.py
+++ b/solution.py
@@ -12,7 +12,7 @@
 ROWS_DEV = 128
 SUPPORT = 8
 CENTRE = SUPPORT // 2
-SLOTS = 128
+SLOTS = 127
 PAIRS = ((0, 0), (0, 1), (0, 2), (1, 1), (1, 2), (2, 2))
 ACROSS_X, ACROSS_Z = 4, 8
 HALF = 48
@@ -21,6 +21,7 @@
 MESH = pl.DeviceIdType.MESH
 F32 = jnp.float32
 BF16 = jnp.bfloat16
+HBM = pltpu.HBM
 
 
 def ring_distance(step, length):
@@ -51,13 +52,23 @@
 
 def kernel(
     chans, n_rows, width,
-    round_ref, row_ref, col_ref, vis_ref, weight_ref, taylor_ref, taps_ref,
-    out_ref, rounds_ref,
-    mine, theirs, a_ref, b_ref, e_ref, cells, mixed, hess_mine, hess_rows, hess_sum, hess_chan,
-    send_sem, recv_sem, row_send, row_recv, hess_send, hess_recv,
+    round_hbm, row_hbm, col_hbm, vis_hbm, weight_hbm, taylor_hbm, taps_hbm,
+    out_hbm, rounds_hbm,
+    round_ref, row_ref, col_ref, vis_ref, weight_ref, taylor_ref, taps_ref, out_ref, rounds_ref,
+    mine, theirs, a_ref, b_ref, e_ref, cells, mixed, hess_mine, hess_rows,
+    in_sem, out_sem, rounds_sem, rows_here, chans_here, send_sem, recv_sem, row_send, row_recv,
 ):
+    inputs = []
+    for i, (src, dst) in enumerate((
+        (weight_hbm, weight_ref), (taylor_hbm, taylor_ref), (col_hbm, col_ref), (round_hbm, round_ref),
+        (vis_hbm, vis_ref), (row_hbm, row_ref), (taps_hbm, taps_ref),
+    )):
+        inputs.append(pltpu.make_async_copy(src, dst, in_sem.at[i]))
+        inputs[-1].start()
+
     me, slab = lax.axis_index("chan"), lax.axis_index("rows")
     my_x, my_z = me // ACROSS_Z, me % ACROSS_Z
+    my_y, core = slab // 2, slab % 2
     steps = near_first()
     half = chans // 2
     n_chan = row_ref.shape[0]
@@ -70,11 +81,36 @@
         return (owner % 2) * half + owner // 2
 
     barrier = pltpu.get_barrier_semaphore()
+    for i in range(1, n_rows // 2):
+        there = (my_y + i) % (n_rows // 2)
+        pl.semaphore_signal(barrier, inc=1, device_id=(me, 2 * there), device_id_type=MESH)
+
+    @pl.when(core == 1)
+    def _():
+        pl.semaphore_signal(barrier, inc=1, device_id=(me, 2 * my_y), device_id_type=MESH)
+
     for step in steps[:0:-1]:
-        pl.semaphore_signal(barrier, inc=1, device_id=(partner(step), slab), device_id_type=MESH)
-    for i in range(1, n_rows):
-        pl.semaphore_signal(barrier, inc=1, device_id=(me, (slab + i) % n_rows), device_id_type=MESH)
-
+        pl.semaphore_signal(barrier, inc=1, device_id=(partner(step), 2 * my_y + 1), device_id_type=MESH)
+
+    inputs[0].wait()
+    inputs[1].wait()
+    weight = weight_ref[...]
+    chan_sum = jnp.sum(weight, axis=1, keepdims=True)
+    on_diagonal = iota((n_chan, n_chan), 0) == iota((n_chan, n_chan), 1)
+    taylor = [
+        jnp.sum(jnp.where(on_diagonal, taylor_ref[t : t + 1, :], 0.0), axis=1, keepdims=True) for t in range(TERMS)
+    ]
+    sublane = iota((8, 128), 0)
+    part = jnp.zeros((8, 128), F32)
+    for i, (a, b) in enumerate(PAIRS):
+        entry = jnp.sum(taylor[a] * taylor[b] * chan_sum, axis=0, keepdims=True)
+        part = jnp.where(sublane == i, entry, part)
+
+    def gather(values):
+        return jnp.where(sublane == len(PAIRS), jnp.max(values, axis=0), jnp.sum(values, axis=0))
+
+    inputs[2].wait()
+    inputs[3].wait()
     col = col_ref[...].astype(F32)
     owner = iota((2 * half, 128), 0)
     owner = jnp.where(owner < half, 2 * owner, 2 * (owner - half) + 1)
@@ -91,9 +127,35 @@
             a_ref[par, 13 * half : 14 * half, n * 128 : n * 128 + 128] = at[par * half : (par + 1) * half]
     before = jnp.where(iota((128, 256), 0) < iota((128, 256), 1), 1.0, 0.0).astype(BF16)
     counts = matmul(e_ref[...], before)
+    fullest = counts[: 2 * half, 128:]
+    for n in range(1, len(pieces)):
+        fullest = fullest + counts[n * 2 * half : (n + 1) * 2 * half, 128:]
+    part = jnp.where(sublane == len(PAIRS), jnp.max(fullest, axis=0, keepdims=True), part)
+    hess_mine[...] = part
+    hess_rows[pl.ds(slab, 1)] = part[None]
+
+    @pl.when(core == 0)
+    def _():
+        pl.semaphore_wait(barrier, n_rows - 1)
+        pl.semaphore_signal(rows_here, inc=1, device_id=(me, slab + 1), device_id_type=MESH)
+
+    @pl.when(core == 1)
+    def _():
+        pl.semaphore_wait(rows_here, 1)
+
+    row_copies = []
+    for i in range(1, n_rows):
+        copy = pltpu.make_async_remote_copy(
+            src_ref=hess_mine, dst_ref=hess_rows.at[slab], send_sem=row_send.at[i], recv_sem=row_recv.at[i],
+            device_id=(me, (slab + i) % n_rows), device_id_type=MESH,
+        )
+        copy.start()
+        row_copies.append(copy)
+
     start = jnp.zeros((2 * half, 128), F32)
     base = (round_ref[0] * SLOTS).astype(F32)
-    slot = iota((SLOTS, 128), 0).astype(F32)
+    slot = iota((128, 128), 0)
+    slot = jnp.where(slot < SLOTS, slot.astype(F32), -0.5)
     for n in range(len(pieces)):
         now = counts[n * 2 * half : (n + 1) * 2 * half]
         rank = reach[n] * (now[:, :128] + start)
@@ -101,27 +163,14 @@
         for par in range(2):
             which = jnp.sum(rank[par * half : (par + 1) * half], axis=0, keepdims=True) - base
             b_ref[par, :, n * 128 : n * 128 + 128] = jnp.where(slot == which, 1.0, 0.0).astype(BF16)
-    fullest = jnp.max(start, axis=0, keepdims=True)
-
-    weight = weight_ref[...]
-    taylor = taylor_ref[...]
-    chan_sum = jnp.sum(weight, axis=1, keepdims=True)
-    lane = iota((1, 128), 1)
-    part = jnp.where(lane == len(PAIRS), fullest, 0.0)
-    for i, (a, b) in enumerate(PAIRS):
-        entry = jnp.sum(taylor[:, a : a + 1] * taylor[:, b : b + 1] * chan_sum, axis=0, keepdims=True)
-        part = part + jnp.where(lane == i, entry, 0.0)
-
-    def gather(values):
-        return jnp.where(lane == len(PAIRS), jnp.max(values, axis=0), jnp.sum(values, axis=0))
-
-    hess_mine[...] = part
-    hess_rows[pl.ds(slab, 1)] = part[None]
-
+
+    inputs[4].wait()
+    inputs[5].wait()
+    inputs[6].wait()
     scaled = []
     for t in range(TERMS):
         for p in range(2):
-            scaled.append(taylor[:, t : t + 1] * (weight * vis_ref[:, p, :]))
+            scaled.append(taylor[t] * (weight * vis_ref[:, p, :]))
     rows = [two_parts(value) for value in scaled]
     rows = [high for high, _ in rows] + [low for _, low in rows] + [row_ref[...].astype(F32).astype(BF16)]
     rows = [value.astype(F32) for value in rows]
@@ -142,41 +191,32 @@
                 value = tile[(6 + i) * half : (7 + i) * half]
             mine[pl.ds(par * half * 8 + i, half, stride=8), :] = value
 
-    pl.semaphore_wait(barrier, chans - 1 + n_rows - 1)
-    row_copies = []
-    for i in range(1, n_rows):
-        to = (slab + i) % n_rows
-        copy = pltpu.make_async_remote_copy(
-            src_ref=hess_mine, dst_ref=hess_rows.at[slab], send_sem=row_send.at[i], recv_sem=row_recv.at[i],
-            device_id=(me, to), device_id_type=MESH,
-        )
-        copy.start()
-        row_copies.append(copy)
+    for copy in row_copies:
+        copy.wait_recv()
+    row_sum = gather(hess_rows[...])
+    last = iota((8, 128), 1) == SLOTS
+    for i in range(chans):
+        mine[i * 8 : i * 8 + 8, :] = jnp.where(last, row_sum, mine[i * 8 : i * 8 + 8, :])
+
+    @pl.when(core == 1)
+    def _():
+        pl.semaphore_wait(barrier, 2 * (chans - 1))
+        pl.semaphore_signal(chans_here, inc=1, device_id=(me, slab - 1), device_id_type=MESH)
+
+    @pl.when(core == 0)
+    def _():
+        pl.semaphore_wait(chans_here, 1)
+
     copies = {}
-    for step in steps[:0:-1]:
-        to = partner(step)
-        i = steps.index(step)
-        copy = pltpu.make_async_remote_copy(
+    for i in range(len(steps) - 1, 0, -1):
+        to = partner(steps[i])
+        copies[i] = pltpu.make_async_remote_copy(
             src_ref=mine.at[pl.ds(pl.multiple_of(place(to) * 8, 8), 8)], dst_ref=theirs.at[i],
             send_sem=send_sem.at[i], recv_sem=recv_sem.at[i],
             device_id=(to, slab), device_id_type=MESH,
         )
-        copy.start()
-        copies[i] = copy
+        copies[i].start()
     theirs[0] = mine[pl.ds(pl.multiple_of(place(me) * 8, 8), 8), :]
-    for copy in row_copies:
-        copy.wait_recv()
-    row_sum = gather(hess_rows[...])
-    hess_sum[...] = row_sum
-    hess_chan[0] = row_sum
-    hess_copies = []
-    for i in range(len(steps) - 1, 0, -1):
-        copy = pltpu.make_async_remote_copy(
-            src_ref=hess_sum, dst_ref=hess_chan.at[i], send_sem=hess_send.at[i], recv_sem=hess_recv.at[i],
-            device_id=(partner(steps[i]), slab), device_id_type=MESH,
-        )
-        copy.start()
-        hess_copies.append(copy)
 
     tap_of = iota((ROWS_DEV, ROWS_DEV), 1) - iota((ROWS_DEV, ROWS_DEV), 0) + CENTRE
     row_taps = jnp.zeros((ROWS_DEV, ROWS_DEV), F32)
@@ -192,6 +232,9 @@
             if i > 0:
                 copies[i].wait_recv()
             tile = theirs[i]
+            sums = tile if i == 0 else sums + tile
+            most = tile if i == 0 else jnp.maximum(most, tile)
+            tile = jnp.where(last, 0.0, tile)
             high = tile.astype(BF16).astype(F32)
             low = tile - high
             at = tile[7:8]
@@ -218,12 +261,9 @@
             matmul(high, row_high) + matmul(low, row_high) + matmul(high, row_low)
         )
 
-    for copy in hess_copies:
-        copy.wait_recv()
-    hess = gather(hess_chan[...])
     entries = {}
     for i, (a, b) in enumerate(PAIRS):
-        entries[a, b] = entries[b, a] = jnp.sum(jnp.where(lane == i, hess, 0.0), axis=1, keepdims=True)
+        entries[a, b] = entries[b, a] = sums[i : i + 1, SLOTS : SLOTS + 1]
     scale = entries[0, 0]
     m = [[entries[a, b] / scale for b in range(3)] for a in range(3)]
 
@@ -233,8 +273,10 @@
     across = [cross(m[1], m[2]), cross(m[2], m[0]), cross(m[0], m[1])]
     det = m[0][0] * across[0][0] + m[0][1] * across[0][1] + m[0][2] * across[0][2]
     inverse = [[across[b][a] / det for b in range(3)] for a in range(3)]
-    count = jnp.max(jnp.where(lane == len(PAIRS), hess, 0.0))
+    count = jnp.max(jnp.where(last & (sublane == len(PAIRS)), most, 0.0))
     rounds_ref[0] = (count.astype(jnp.int32) + (SLOTS - 1)) // SLOTS
+    rounds_copy = pltpu.make_async_copy(rounds_ref, rounds_hbm, rounds_sem)
+    rounds_copy.start()
 
     wide = width // 2
     col_taps = [jnp.full((8, 128), taps_ref[j], F32).astype(BF16).astype(F32)[:1] for j in range(SUPPORT)]
@@ -252,39 +294,47 @@
                 value = inverse[a][0] * grids[0] + inverse[a][1] * grids[1] + inverse[a][2] * grids[2]
                 out_ref[pl.ds(e * 6 + a * 2 + p, wide, stride=12), :] = value
 
-    for copy in row_copies + hess_copies + list(copies.values()):
+    out_copy = pltpu.make_async_copy(out_ref, out_hbm, out_sem)
+    out_copy.start()
+    for copy in row_copies + list(copies.values()):
         copy.wait_send()
+    rounds_copy.wait()
+    out_copy.wait()
 
 
 def grid_round(chans, n_rows, width, which, arrays):
-    vmem, smem = pl.BlockSpec(memory_space=pltpu.VMEM), pl.BlockSpec(memory_space=pltpu.SMEM)
+    hbm = pl.BlockSpec(memory_space=HBM)
     n_vis = arrays[0].shape[0] * arrays[0].shape[1]
+    out = jax.ShapeDtypeStruct((width * TERMS * 2, ROWS_DEV), F32)
     return pl.pallas_call(
         functools.partial(kernel, chans, n_rows, width),
-        out_shape=(
-            jax.ShapeDtypeStruct((width * TERMS * 2, ROWS_DEV), F32),
-            jax.ShapeDtypeStruct((1,), jnp.int32),
-        ),
-        in_specs=[smem] + [vmem] * 5 + [smem],
-        out_specs=(vmem, smem),
+        out_shape=(out, jax.ShapeDtypeStruct((1,), jnp.int32)),
+        in_specs=[hbm] * 7,
+        out_specs=(hbm, hbm),
         scratch_shapes=[
-            pltpu.VMEM((chans * 8, SLOTS), F32),
-            pltpu.VMEM((chans, 8, SLOTS), F32),
+            pltpu.SMEM((1,), jnp.int32),
+            *[pltpu.VMEM(a.shape, a.dtype) for a in arrays[:-1]],
+            pltpu.SMEM(arrays[-1].shape, F32),
+            pltpu.VMEM(out.shape, F32),
+            pltpu.SMEM((1,), jnp.int32),
+            pltpu.VMEM((chans * 8, 128), F32),
+            pltpu.VMEM((chans, 8, 128), F32),
             pltpu.VMEM((2, 14 * chans // 2, n_vis), BF16),
-            pltpu.VMEM((2, SLOTS, n_vis), BF16),
+            pltpu.VMEM((2, 128, n_vis), BF16),
             pltpu.VMEM((n_vis // 128 * chans, 128), BF16),
             pltpu.VMEM((12 * HALF, 2 * ROWS_DEV), F32),
             pltpu.VMEM((12 * HALF, ROWS_DEV), F32),
-            pltpu.VMEM((1, 128), F32),
-            pltpu.VMEM((n_rows, 1, 128), F32),
-            pltpu.VMEM((1, 128), F32),
-            pltpu.VMEM((chans, 1, 128), F32),
+            pltpu.VMEM((8, 128), F32),
+            pltpu.VMEM((n_rows, 8, 128), F32),
+            pltpu.SemaphoreType.DMA((7,)),
+            pltpu.SemaphoreType.DMA,
+            pltpu.SemaphoreType.DMA,
+            pltpu.SemaphoreType.REGULAR,
+            pltpu.SemaphoreType.REGULAR,
             pltpu.SemaphoreType.DMA((chans,)),
             pltpu.SemaphoreType.DMA((chans,)),
             pltpu.SemaphoreType.DMA((n_rows,)),
             pltpu.SemaphoreType.DMA((n_rows,)),
-            pltpu.SemaphoreType.DMA((chans,)),
-            pltpu.SemaphoreType.DMA((chans,)),
         ],
         compiler_params=pltpu.CompilerParams(
             collective_id=0, has_side_effects=True, vmem_limit_bytes=40 * 1024 * 1024
@@ -292,7 +342,8 @@
     )(which, *arrays)
 
 
-def body(*arrays):
+def body(row_cells, col_cells, visibilities, imaging_weights, taylor_weights, kernel_taps):
+    arrays = (row_cells, col_cells, visibilities, imaging_weights, taylor_weights.T, kernel_taps)
     chans, n_rows = lax.axis_size("chan"), lax.axis_size("rows")
     width = NCOL // chans
 

time: 24.9 us -> 23.6 us (0.948)
  Pallas kernels: 22.5 us -> 21.4 us
    pallas_call x1, Pallas kernels: 22.5 us -> 21.4 us  [grid_round(): pl.pallas_call(functools.partial(kernel, chans, n_rows, width), out_shape...]
    unnamed x12 -> x13, local copies, waits for them, and re-layouts: 1.47 us -> 1.38 us
where the time goes in v2:
time: 23.6 us; the launch traced here: 23.5 us
  Pallas kernels  21.4 us (91%)
  local copies, waits for them, and re-layouts  1.38 us (6%)
  loops' own time  0.63 us (3%)
    pallas_call x1, Pallas kernels, grid_round(): pl.pallas_call(functools.partial(kernel, chans, n_rows, width), out_shape...  21.4 us
    unnamed x13, local copies, waits for them, and re-layouts  1.38 us
    another operation x1, loops' own time, body(): _, _, total = lax.while_loop(more, step, (jnp.int32(1), rounds[0], part))  0.63 us

profile of v2, /device:TPU:1, one launch (start us, length us, event | category | flops | bytes accessed | tf_op | source)
XLA Modules:
  0.0 23.5 jit_solution(17540757892955458207)
XLA Ops:
  0.0 0.0 copy-start.4
  0.0 0.0 copy-start.5
  0.0 0.7 %copy-done.4 = f32[8,3]{0,1:T(4,128)S(1)} copy-done((f32[8,3]{0,1:T(4,128)S(1)}, f32[8,3]{0,1:T(4,128)}, u32[]{:S(2)}) %copy-start.4) | copy-done | bytes 120
  0.7 0.0 copy-done.5
  0.7 0.0 copy-start
  0.7 0.0 copy-start.1
  0.7 0.0 copy-start.2
  0.7 0.0 copy-start.3
  0.7 21.4 %shard_map.64 = (f32[384,128]{1,0:T(8,128)S(1)}, s32[1]{0:T(128)}) custom-call(s32[1]{0:T(128)} %constant.2.clone.1.round_hbm, s32[8,256]{1,0:T(8,128)} %row_hbm.1, s32[8,256]{1,0:T(8,128)} %col_hbm.1, f32[8,2,256]{2,1,0:T(2,128)} %vis_hbm.1, f32[8,256]{1,0:T(8,128)} %weight_hbm.1, f32[3,8]{1,0:T(4,128)S(1)} %bitcast.10, f32[8]{0:T(128)S(1)} %copy-done.5), custom_call_target="tpu_custom_call" | custom-call | tf_op jit(solution)/shard_map/pallas_call | solution.py:309
  22.1 0.0 copy-done
  22.1 0.0 copy-done.1
  22.1 0.0 copy-done.2
  22.2 0.0 copy-done.3
  22.2 0.6 %while.12 = (s32[]{:T(128)}, s32[]{:T(128)}, f32[384,128]{1,0:T(8,128)S(1)}, s32[8,256]{1,0:T(8,128)S(1)}, s32[8,256]{1,0:T(8,128)S(1)}, /*index=5*/f32[8,2,256]...) while((s32[]{:T(128)}, s32[]{:T(128)}, f32[384,128]{1,0:T(8,128)S(1)}, ...), condition=%wide.region_1.0_spmd, body=%wide.region_0.0_spmd.sunk | while | flops 49154 | bytes 589933 | solution.py:359
  22.8 0.7 %copy.17 = f32[64,3,2,128]{3,2,1,0:T(2,128)} copy(f32[64,3,2,128]{3,2,1,0:T(2,128)S(1)} %bitcast.9) | data formatting | bytes 393216
Async XLA Ops:
  0.0 0.7 %copy-start.4 = (f32[8,3]{0,1:T(4,128)S(1)}, f32[8,3]{0,1:T(4,128)}, u32[]{:S(2)}) copy-start(f32[8,3]{0,1:T(4,128)} %param.12) | copy-start | bytes 292
  0.0 0.7 %copy-start.5 = (f32[8]{0:T(128)S(1)}, f32[8]{0:T(128)}, u32[]{:S(2)}) copy-start(f32[8]{0:T(128)} %taps_hbm.1) | copy-start | bytes 100
  0.7 21.4 %copy-start = (f32[8,2,256]{2,1,0:T(2,128)S(1)}, f32[8,2,256]{2,1,0:T(2,128)}, u32[]{:S(2)}) copy-start(f32[8,2,256]{2,1,0:T(2,128)} %vis_hbm.1) | copy-start | bytes 49156
  0.7 21.4 %copy-start.1 = (s32[8,256]{1,0:T(8,128)S(1)}, s32[8,256]{1,0:T(8,128)}, u32[]{:S(2)}) copy-start(s32[8,256]{1,0:T(8,128)} %row_hbm.1) | copy-start | bytes 24580
  0.7 21.5 %copy-start.2 = (s32[8,256]{1,0:T(8,128)S(1)}, s32[8,256]{1,0:T(8,128)}, u32[]{:S(2)}) copy-start(s32[8,256]{1,0:T(8,128)} %col_hbm.1) | copy-start | bytes 24580
  0.7 21.5 %copy-start.3 = (f32[8,256]{1,0:T(8,128)S(1)}, f32[8,256]{1,0:T(8,128)}, u32[]{:S(2)}) copy-start(f32[8,256]{1,0:T(8,128)} %weight_hbm.1) | copy-start | bytes 24580

commit v3 on v2

--- a/solution.py
+++ b/solution.py
@@ -15,6 +15,7 @@
 SLOTS = 127
 PAIRS = ((0, 0), (0, 1), (0, 2), (1, 1), (1, 2), (2, 2))
 ACROSS_X, ACROSS_Z = 4, 8
+Z_ORDER = (0, 1, 2, 3, 7, 6, 5, 4)
 HALF = 48
 PER_STEP = 4
 
@@ -24,13 +25,8 @@
 HBM = pltpu.HBM
 
 
-def ring_distance(step, length):
-    return min(step % length, -step % length)
-
-
-def near_first():
-    steps = [(x, z) for x in range(ACROSS_X) for z in range(ACROSS_Z)]
-    return sorted(steps, key=lambda s: (ring_distance(s[0], ACROSS_X) + ring_distance(s[1], ACROSS_Z), s))
+def in_order_of_start():
+    return [x * ACROSS_Z + z for z in Z_ORDER for x in range(ACROSS_X)]
 
 
 def matmul_nt(a, b):
@@ -53,10 +49,10 @@
 def kernel(
     chans, n_rows, width,
     round_hbm, row_hbm, col_hbm, vis_hbm, weight_hbm, taylor_hbm, taps_hbm,
-    out_hbm, rounds_hbm,
-    round_ref, row_ref, col_ref, vis_ref, weight_ref, taylor_ref, taps_ref, out_ref, rounds_ref,
+    out_ref, rounds_ref,
+    round_ref, row_ref, col_ref, vis_ref, weight_ref, taylor_ref, taps_ref,
     mine, theirs, a_ref, b_ref, e_ref, cells, mixed, hess_mine, hess_rows,
-    in_sem, out_sem, rounds_sem, rows_here, chans_here, send_sem, recv_sem, row_send, row_recv,
+    in_sem, rows_here, chans_here, send_sem, recv_sem, row_send, row_recv,
 ):
     inputs = []
     for i, (src, dst) in enumerate((
@@ -67,15 +63,11 @@
         inputs[-1].start()
 
     me, slab = lax.axis_index("chan"), lax.axis_index("rows")
-    my_x, my_z = me // ACROSS_Z, me % ACROSS_Z
     my_y, core = slab // 2, slab % 2
-    steps = near_first()
+    chips = in_order_of_start()
     half = chans // 2
     n_chan = row_ref.shape[0]
     pieces = [(c, h) for c in range(n_chan) for h in range(2)]
-
-    def partner(step):
-        return ((my_x + step[0]) % ACROSS_X) * ACROSS_Z + (my_z + step[1]) % ACROSS_Z
 
     def place(owner):
         return (owner % 2) * half + owner // 2
@@ -89,8 +81,11 @@
     def _():
         pl.semaphore_signal(barrier, inc=1, device_id=(me, 2 * my_y), device_id_type=MESH)
 
-    for step in steps[:0:-1]:
-        pl.semaphore_signal(barrier, inc=1, device_id=(partner(step), 2 * my_y + 1), device_id_type=MESH)
+    for chip in chips:
+
+        @pl.when(chip != me)
+        def _(chip=chip):
+            pl.semaphore_signal(barrier, inc=1, device_id=(chip, 2 * my_y + 1), device_id_type=MESH)
 
     inputs[0].wait()
     inputs[1].wait()
@@ -207,16 +202,27 @@
     def _():
         pl.semaphore_wait(chans_here, 1)
 
-    copies = {}
-    for i in range(len(steps) - 1, 0, -1):
-        to = partner(steps[i])
-        copies[i] = pltpu.make_async_remote_copy(
-            src_ref=mine.at[pl.ds(pl.multiple_of(place(to) * 8, 8), 8)], dst_ref=theirs.at[i],
-            send_sem=send_sem.at[i], recv_sem=recv_sem.at[i],
-            device_id=(to, slab), device_id_type=MESH,
+    def tile_to(owner):
+        return pltpu.make_async_remote_copy(
+            src_ref=mine.at[pl.ds(place(owner) * 8, 8)], dst_ref=theirs.at[me],
+            send_sem=send_sem.at[owner], recv_sem=recv_sem.at[me],
+            device_id=(owner, slab), device_id_type=MESH,
         )
-        copies[i].start()
-    theirs[0] = mine[pl.ds(pl.multiple_of(place(me) * 8, 8), 8), :]
+
+    def tile_from(sender):
+        return pltpu.make_async_remote_copy(
+            src_ref=mine.at[pl.ds(0, 8)], dst_ref=theirs.at[sender],
+            send_sem=send_sem.at[sender], recv_sem=recv_sem.at[sender],
+            device_id=(sender, slab), device_id_type=MESH,
+        )
+
+    for chip in chips:
+
+        @pl.when(chip != me)
+        def _(chip=chip):
+            tile_to(chip).start()
+
+    theirs[me] = mine[pl.ds(pl.multiple_of(place(me) * 8, 8), 8), :]
 
     tap_of = iota((ROWS_DEV, ROWS_DEV), 1) - iota((ROWS_DEV, ROWS_DEV), 0) + CENTRE
     row_taps = jnp.zeros((ROWS_DEV, ROWS_DEV), F32)
@@ -226,14 +232,18 @@
 
     half_cell = iota((HALF, 128), 0).astype(F32)
     row_cell = iota((2 * ROWS_DEV, 128), 0).astype(F32)
-    for g in range(0, len(steps), PER_STEP):
+    for g in range(0, chans, PER_STEP):
         a_parts, b_parts = [], []
-        for i in range(g, g + PER_STEP):
-            if i > 0:
-                copies[i].wait_recv()
+        for chip in chips[g : g + PER_STEP]:
+
+            @pl.when(chip != me)
+            def _(chip=chip):
+                tile_from(chip).wait_recv()
+
+        for i in chips[g : g + PER_STEP]:
             tile = theirs[i]
-            sums = tile if i == 0 else sums + tile
-            most = tile if i == 0 else jnp.maximum(most, tile)
+            sums = tile if i == chips[0] else sums + tile
+            most = tile if i == chips[0] else jnp.maximum(most, tile)
             tile = jnp.where(last, 0.0, tile)
             high = tile.astype(BF16).astype(F32)
             low = tile - high
@@ -275,8 +285,6 @@
     inverse = [[across[b][a] / det for b in range(3)] for a in range(3)]
     count = jnp.max(jnp.where(last & (sublane == len(PAIRS)), most, 0.0))
     rounds_ref[0] = (count.astype(jnp.int32) + (SLOTS - 1)) // SLOTS
-    rounds_copy = pltpu.make_async_copy(rounds_ref, rounds_hbm, rounds_sem)
-    rounds_copy.start()
 
     wide = width // 2
     col_taps = [jnp.full((8, 128), taps_ref[j], F32).astype(BF16).astype(F32)[:1] for j in range(SUPPORT)]
@@ -294,12 +302,13 @@
                 value = inverse[a][0] * grids[0] + inverse[a][1] * grids[1] + inverse[a][2] * grids[2]
                 out_ref[pl.ds(e * 6 + a * 2 + p, wide, stride=12), :] = value
 
-    out_copy = pltpu.make_async_copy(out_ref, out_hbm, out_sem)
-    out_copy.start()
-    for copy in row_copies + list(copies.values()):
+    for copy in row_copies:
         copy.wait_send()
-    rounds_copy.wait()
-    out_copy.wait()
+    for chip in chips:
+
+        @pl.when(chip != me)
+        def _(chip=chip):
+            tile_to(chip).wait_send()
 
 
 def grid_round(chans, n_rows, width, which, arrays):
@@ -308,15 +317,13 @@
     out = jax.ShapeDtypeStruct((width * TERMS * 2, ROWS_DEV), F32)
     return pl.pallas_call(
         functools.partial(kernel, chans, n_rows, width),
-        out_shape=(out, jax.ShapeDtypeStruct((1,), jnp.int32)),
+        out_shape=(pltpu.VMEM(out.shape, F32), pltpu.SMEM((1,), jnp.int32)),
         in_specs=[hbm] * 7,
-        out_specs=(hbm, hbm),
+        out_specs=(pl.BlockSpec(memory_space=pltpu.VMEM), pl.BlockSpec(memory_space=pltpu.SMEM)),
         scratch_shapes=[
             pltpu.SMEM((1,), jnp.int32),
             *[pltpu.VMEM(a.shape, a.dtype) for a in arrays[:-1]],
             pltpu.SMEM(arrays[-1].shape, F32),
-            pltpu.VMEM(out.shape, F32),
-            pltpu.SMEM((1,), jnp.int32),
             pltpu.VMEM((chans * 8, 128), F32),
             pltpu.VMEM((chans, 8, 128), F32),
             pltpu.VMEM((2, 14 * chans // 2, n_vis), BF16),
@@ -327,8 +334,6 @@
             pltpu.VMEM((8, 128), F32),
             pltpu.VMEM((n_rows, 8, 128), F32),
             pltpu.SemaphoreType.DMA((7,)),
-            pltpu.SemaphoreType.DMA,
-            pltpu.SemaphoreType.DMA,
             pltpu.SemaphoreType.REGULAR,
             pltpu.SemaphoreType.REGULAR,
             pltpu.SemaphoreType.DMA((chans,)),
@@ -339,7 +344,7 @@
         compiler_params=pltpu.CompilerParams(
             collective_id=0, has_side_effects=True, vmem_limit_bytes=40 * 1024 * 1024
         ),
-    )(which, *arrays)
+    )(*[pltpu.with_memory_space_constraint(a, HBM) for a in (which, *arrays)])
 
 
 def body(row_cells, col_cells, visibilities, imaging_weights, taylor_weights, kernel_taps):

time: 23.6 us -> 20.5 us (0.87); the launches traced: 23.5 us -> 20.1 us
  Pallas kernels: 21.4 us -> 19.4 us
  local copies, waits for them, and re-layouts: 1.38 us -> 0.68 us
  loops' own time: 0.63 us -> 0.01 us
    pallas_call x1, Pallas kernels: 21.4 us -> 19.4 us  [grid_round(): pl.pallas_call(functools.partial(kernel, chans, n_rows, width), out_shape...]
    unnamed x13 -> x1, local copies, waits for them, and re-layouts: 1.38 us -> 0.68 us
    another operation x1, loops' own time: 0.63 us -> 0.01 us  [body(): _, _, total = lax.while_loop(more, step, (jnp.int32(1), rounds[0], part))]
where the time goes in v3:
time: 20.5 us; the launch traced here: 20.1 us
  Pallas kernels  19.4 us (95%)
  local copies, waits for them, and re-layouts  0.68 us (3%)
    pallas_call x1, Pallas kernels, grid_round(): pl.pallas_call(functools.partial(kernel, chans, n_rows, width), out_shape...  19.4 us
    unnamed x1, local copies, waits for them, and re-layouts  0.68 us

profile of v3, /device:TPU:1, one launch (start us, length us, event | category | flops | bytes accessed | tf_op | source)
XLA Modules:
  0.0 20.1 jit_solution(1505252825719546609)
XLA Ops:
  0.0 19.4 %shard_map.64 = (f32[384,128]{1,0:T(8,128)S(1)}, s32[1]{0:T(128)S(4)}) custom-call(s32[1]{0:T(128)} %constant.2.clone.1.round_hbm, s32[8,256]{1,0:T(8,128)} %row_hbm.1, s32[8,256]{1,0:T(8,128)} %col_hbm.1, f32[8,2,256]{2,1,0:T(2,128)} %vis_hbm.1, f32[8,256]{1,0:T(8,128)} %weight_hbm.1, f32[3,8]{1,0:T(4,128)} %bitcast.10, f32[8]{0:T(128)} %taps_hbm.1), custom_call_target="tpu_custom_call" | custom-call | tf_op jit(solution)/shard_map/pallas_call | solution.py:318
  19.5 0.7 %copy.17 = f32[64,3,2,128]{3,2,1,0:T(2,128)} copy(f32[64,3,2,128]{3,2,1,0:T(2,128)S(1)} %bitcast.9) | data formatting | bytes 393216
  (1 shorter events, 0.0 us)

commit v4 on v3

--- a/solution.py
+++ b/solution.py
@@ -12,10 +12,11 @@
 ROWS_DEV = 128
 SUPPORT = 8
 CENTRE = SUPPORT // 2
-SLOTS = 127
+SLOTS = 128
 PAIRS = ((0, 0), (0, 1), (0, 2), (1, 1), (1, 2), (2, 2))
 ACROSS_X, ACROSS_Z = 4, 8
 Z_ORDER = (0, 1, 2, 3, 7, 6, 5, 4)
+EARLY = 3
 HALF = 48
 PER_STEP = 4
 
@@ -51,17 +52,9 @@
     round_hbm, row_hbm, col_hbm, vis_hbm, weight_hbm, taylor_hbm, taps_hbm,
     out_ref, rounds_ref,
     round_ref, row_ref, col_ref, vis_ref, weight_ref, taylor_ref, taps_ref,
-    mine, theirs, a_ref, b_ref, e_ref, cells, mixed, hess_mine, hess_rows,
-    in_sem, rows_here, chans_here, send_sem, recv_sem, row_send, row_recv,
+    mine, theirs, a_ref, b_ref, e_ref, cells, mixed, grids, hess_mine, hess_chan, hess_sum, hess_rows,
+    in_sem, early_here, late_here, send_sem, recv_sem, row_send, row_recv, hess_send, hess_recv,
 ):
-    inputs = []
-    for i, (src, dst) in enumerate((
-        (weight_hbm, weight_ref), (taylor_hbm, taylor_ref), (col_hbm, col_ref), (round_hbm, round_ref),
-        (vis_hbm, vis_ref), (row_hbm, row_ref), (taps_hbm, taps_ref),
-    )):
-        inputs.append(pltpu.make_async_copy(src, dst, in_sem.at[i]))
-        inputs[-1].start()
-
     me, slab = lax.axis_index("chan"), lax.axis_index("rows")
     my_y, core = slab // 2, slab % 2
     chips = in_order_of_start()
@@ -72,40 +65,33 @@
     def place(owner):
         return (owner % 2) * half + owner // 2
 
+    inputs = []
+    for i, (src, dst) in enumerate((
+        (col_hbm, col_ref), (round_hbm, round_ref), (weight_hbm, weight_ref), (taylor_hbm, taylor_ref),
+        (vis_hbm, vis_ref), (row_hbm, row_ref), (taps_hbm, taps_ref),
+    )):
+        inputs.append(pltpu.make_async_copy(src, dst, in_sem.at[i]))
+        inputs[-1].start()
+
+    is_early = me % ACROSS_Z < EARLY
+    others = chans // ACROSS_Z * EARLY * 2
+    n_early = others + 1 - 2 * is_early.astype(jnp.int32)
+    n_late = 2 * chans - others - 2 + 2 * is_early.astype(jnp.int32) + n_rows - 1
     barrier = pltpu.get_barrier_semaphore()
+    counter = 2 * my_y + 1 - is_early.astype(jnp.int32)
+    for chip in chips[::-1]:
+
+        @pl.when(chip != me)
+        def _(chip=chip):
+            pl.semaphore_signal(barrier, inc=1, device_id=(chip, counter), device_id_type=MESH)
+
     for i in range(1, n_rows // 2):
         there = (my_y + i) % (n_rows // 2)
-        pl.semaphore_signal(barrier, inc=1, device_id=(me, 2 * there), device_id_type=MESH)
-
-    @pl.when(core == 1)
-    def _():
-        pl.semaphore_signal(barrier, inc=1, device_id=(me, 2 * my_y), device_id_type=MESH)
-
-    for chip in chips:
-
-        @pl.when(chip != me)
-        def _(chip=chip):
-            pl.semaphore_signal(barrier, inc=1, device_id=(chip, 2 * my_y + 1), device_id_type=MESH)
+        pl.semaphore_signal(barrier, inc=1, device_id=(me, 2 * there + 1), device_id_type=MESH)
+    pl.semaphore_signal(barrier, inc=1, device_id=(me, slab + 1 - 2 * core), device_id_type=MESH)
 
     inputs[0].wait()
     inputs[1].wait()
-    weight = weight_ref[...]
-    chan_sum = jnp.sum(weight, axis=1, keepdims=True)
-    on_diagonal = iota((n_chan, n_chan), 0) == iota((n_chan, n_chan), 1)
-    taylor = [
-        jnp.sum(jnp.where(on_diagonal, taylor_ref[t : t + 1, :], 0.0), axis=1, keepdims=True) for t in range(TERMS)
-    ]
-    sublane = iota((8, 128), 0)
-    part = jnp.zeros((8, 128), F32)
-    for i, (a, b) in enumerate(PAIRS):
-        entry = jnp.sum(taylor[a] * taylor[b] * chan_sum, axis=0, keepdims=True)
-        part = jnp.where(sublane == i, entry, part)
-
-    def gather(values):
-        return jnp.where(sublane == len(PAIRS), jnp.max(values, axis=0), jnp.sum(values, axis=0))
-
-    inputs[2].wait()
-    inputs[3].wait()
     col = col_ref[...].astype(F32)
     owner = iota((2 * half, 128), 0)
     owner = jnp.where(owner < half, 2 * owner, 2 * (owner - half) + 1)
@@ -125,32 +111,58 @@
     fullest = counts[: 2 * half, 128:]
     for n in range(1, len(pieces)):
         fullest = fullest + counts[n * 2 * half : (n + 1) * 2 * half, 128:]
-    part = jnp.where(sublane == len(PAIRS), jnp.max(fullest, axis=0, keepdims=True), part)
+    inputs[2].wait()
+    inputs[3].wait()
+    weight = weight_ref[...]
+    weight_sum = jnp.sum(weight, axis=1, keepdims=True)
+    on_diagonal = iota((n_chan, n_chan), 0) == iota((n_chan, n_chan), 1)
+    taylor = [
+        jnp.sum(jnp.where(on_diagonal, taylor_ref[t : t + 1, :], 0.0), axis=1, keepdims=True) for t in range(TERMS)
+    ]
+    lane = iota((1, 128), 1)
+    part = jnp.where(lane == len(PAIRS), jnp.max(fullest, axis=0, keepdims=True), 0.0)
+    for i, (a, b) in enumerate(PAIRS):
+        entry = jnp.sum(taylor[a] * taylor[b] * weight_sum, axis=0, keepdims=True)
+        part = jnp.where(lane == i, entry, part)
     hess_mine[...] = part
-    hess_rows[pl.ds(slab, 1)] = part[None]
+    hess_chan[pl.ds(me, 1)] = part[None]
+
+    def gather(values):
+        return jnp.where(lane == len(PAIRS), jnp.max(values, axis=0), jnp.sum(values, axis=0))
+
+    def part_with(partner, sender):
+        return pltpu.make_async_remote_copy(
+            src_ref=hess_mine, dst_ref=hess_chan.at[sender], send_sem=hess_send, recv_sem=hess_recv,
+            device_id=(partner, slab), device_id_type=MESH,
+        )
+
+    all_parts = pltpu.make_async_remote_copy(
+        src_ref=hess_chan.at[pl.ds(0, chans - 1)], dst_ref=hess_chan.at[pl.ds(0, chans - 1)],
+        send_sem=hess_send, recv_sem=hess_recv, device_id=(me, slab), device_id_type=MESH,
+    )
+
+    def to_chips(early, start):
+        for chip in chips:
+            if (chip % ACROSS_Z < EARLY) == early:
+
+                @pl.when(chip != me)
+                def _(chip=chip):
+                    start(chip)
 
     @pl.when(core == 0)
     def _():
-        pl.semaphore_wait(barrier, n_rows - 1)
-        pl.semaphore_signal(rows_here, inc=1, device_id=(me, slab + 1), device_id_type=MESH)
+        pl.semaphore_wait(barrier, n_early)
+        pl.semaphore_signal(early_here, inc=1, device_id=(me, slab + 1), device_id_type=MESH)
 
     @pl.when(core == 1)
     def _():
-        pl.semaphore_wait(rows_here, 1)
-
-    row_copies = []
-    for i in range(1, n_rows):
-        copy = pltpu.make_async_remote_copy(
-            src_ref=hess_mine, dst_ref=hess_rows.at[slab], send_sem=row_send.at[i], recv_sem=row_recv.at[i],
-            device_id=(me, (slab + i) % n_rows), device_id_type=MESH,
-        )
-        copy.start()
-        row_copies.append(copy)
+        pl.semaphore_wait(early_here, 1)
+
+    to_chips(True, lambda chip: part_with(chip, me).start())
 
     start = jnp.zeros((2 * half, 128), F32)
     base = (round_ref[0] * SLOTS).astype(F32)
-    slot = iota((128, 128), 0)
-    slot = jnp.where(slot < SLOTS, slot.astype(F32), -0.5)
+    slot = iota((SLOTS, 128), 0).astype(F32)
     for n in range(len(pieces)):
         now = counts[n * 2 * half : (n + 1) * 2 * half]
         rank = reach[n] * (now[:, :128] + start)
@@ -186,42 +198,33 @@
                 value = tile[(6 + i) * half : (7 + i) * half]
             mine[pl.ds(par * half * 8 + i, half, stride=8), :] = value
 
-    for copy in row_copies:
-        copy.wait_recv()
-    row_sum = gather(hess_rows[...])
-    last = iota((8, 128), 1) == SLOTS
-    for i in range(chans):
-        mine[i * 8 : i * 8 + 8, :] = jnp.where(last, row_sum, mine[i * 8 : i * 8 + 8, :])
-
-    @pl.when(core == 1)
-    def _():
-        pl.semaphore_wait(barrier, 2 * (chans - 1))
-        pl.semaphore_signal(chans_here, inc=1, device_id=(me, slab - 1), device_id_type=MESH)
-
-    @pl.when(core == 0)
-    def _():
-        pl.semaphore_wait(chans_here, 1)
-
     def tile_to(owner):
         return pltpu.make_async_remote_copy(
             src_ref=mine.at[pl.ds(place(owner) * 8, 8)], dst_ref=theirs.at[me],
-            send_sem=send_sem.at[owner], recv_sem=recv_sem.at[me],
+            send_sem=send_sem, recv_sem=recv_sem.at[me],
             device_id=(owner, slab), device_id_type=MESH,
         )
 
     def tile_from(sender):
         return pltpu.make_async_remote_copy(
             src_ref=mine.at[pl.ds(0, 8)], dst_ref=theirs.at[sender],
-            send_sem=send_sem.at[sender], recv_sem=recv_sem.at[sender],
+            send_sem=send_sem, recv_sem=recv_sem.at[sender],
             device_id=(sender, slab), device_id_type=MESH,
         )
 
-    for chip in chips:
-
-        @pl.when(chip != me)
-        def _(chip=chip):
-            tile_to(chip).start()
-
+    to_chips(True, lambda chip: tile_to(chip).start())
+
+    @pl.when(core == 1)
+    def _():
+        pl.semaphore_wait(barrier, n_late)
+        pl.semaphore_signal(late_here, inc=1, device_id=(me, slab - 1), device_id_type=MESH)
+
+    @pl.when(core == 0)
+    def _():
+        pl.semaphore_wait(late_here, 1)
+
+    to_chips(False, lambda chip: part_with(chip, me).start())
+    to_chips(False, lambda chip: tile_to(chip).start())
     theirs[me] = mine[pl.ds(pl.multiple_of(place(me) * 8, 8), 8), :]
 
     tap_of = iota((ROWS_DEV, ROWS_DEV), 1) - iota((ROWS_DEV, ROWS_DEV), 0) + CENTRE
@@ -232,19 +235,17 @@
 
     half_cell = iota((HALF, 128), 0).astype(F32)
     row_cell = iota((2 * ROWS_DEV, 128), 0).astype(F32)
-    for g in range(0, chans, PER_STEP):
-        a_parts, b_parts = [], []
+    def arrived(g):
         for chip in chips[g : g + PER_STEP]:
 
             @pl.when(chip != me)
             def _(chip=chip):
                 tile_from(chip).wait_recv()
 
+    def grid_step(g):
+        a_parts, b_parts = [], []
         for i in chips[g : g + PER_STEP]:
             tile = theirs[i]
-            sums = tile if i == chips[0] else sums + tile
-            most = tile if i == chips[0] else jnp.maximum(most, tile)
-            tile = jnp.where(last, 0.0, tile)
             high = tile.astype(BF16).astype(F32)
             low = tile - high
             at = tile[7:8]
@@ -264,6 +265,23 @@
         else:
             cells[...] += total
 
+    all_parts.wait_recv()
+    chan_sum = gather(hess_chan[...])
+    hess_sum[...] = chan_sum
+    hess_rows[pl.ds(slab, 1)] = chan_sum[None]
+    row_copies = []
+    for i in range(1, n_rows):
+        copy = pltpu.make_async_remote_copy(
+            src_ref=hess_sum, dst_ref=hess_rows.at[slab], send_sem=row_send.at[i], recv_sem=row_recv.at[i],
+            device_id=(me, (slab + i) % n_rows), device_id_type=MESH,
+        )
+        copy.start()
+        row_copies.append(copy)
+
+    for g in range(0, chans, PER_STEP):
+        arrived(g)
+        grid_step(g)
+
     for par in range(2):
         x = cells[: 6 * HALF, par * 128 : par * 128 + 128] + cells[6 * HALF :, par * 128 : par * 128 + 128]
         high, low = two_parts(x)
@@ -271,9 +289,29 @@
             matmul(high, row_high) + matmul(low, row_high) + matmul(high, row_low)
         )
 
+    wide = width // 2
+    col_taps = [jnp.full((8, 128), taps_ref[j], F32).astype(BF16).astype(F32)[:1] for j in range(SUPPORT)]
+    for e in range(2):
+        for tp in range(2 * TERMS):
+            grid = jnp.zeros((wide, 128), F32)
+            for j in range(SUPPORT):
+                shift = e + SUPPORT - 1 - j
+                at = ((shift % 2) * 6 + tp) * HALF + shift // 2
+                grid = grid + col_taps[j] * mixed[at : at + wide, :]
+            grids[e, tp] = grid
+
+    all_parts.wait_send()
+    pltpu.make_async_remote_copy(
+        src_ref=theirs.at[pl.ds(0, chans - 1)], dst_ref=theirs.at[pl.ds(0, chans - 1)],
+        send_sem=send_sem, recv_sem=recv_sem.at[0], device_id=(me, slab), device_id_type=MESH,
+    ).wait_send()
+
+    for copy in row_copies:
+        copy.wait()
+    hess = gather(hess_rows[...])
     entries = {}
     for i, (a, b) in enumerate(PAIRS):
-        entries[a, b] = entries[b, a] = sums[i : i + 1, SLOTS : SLOTS + 1]
+        entries[a, b] = entries[b, a] = jnp.sum(jnp.where(lane == i, hess, 0.0), axis=1, keepdims=True)
     scale = entries[0, 0]
     m = [[entries[a, b] / scale for b in range(3)] for a in range(3)]
 
@@ -283,32 +321,15 @@
     across = [cross(m[1], m[2]), cross(m[2], m[0]), cross(m[0], m[1])]
     det = m[0][0] * across[0][0] + m[0][1] * across[0][1] + m[0][2] * across[0][2]
     inverse = [[across[b][a] / det for b in range(3)] for a in range(3)]
-    count = jnp.max(jnp.where(last & (sublane == len(PAIRS)), most, 0.0))
+    count = jnp.max(jnp.where(lane == len(PAIRS), hess, 0.0))
     rounds_ref[0] = (count.astype(jnp.int32) + (SLOTS - 1)) // SLOTS
 
-    wide = width // 2
-    col_taps = [jnp.full((8, 128), taps_ref[j], F32).astype(BF16).astype(F32)[:1] for j in range(SUPPORT)]
     for e in range(2):
         for p in range(2):
-            grids = []
-            for t in range(TERMS):
-                grid = jnp.zeros((wide, 128), F32)
-                for j in range(SUPPORT):
-                    shift = e + SUPPORT - 1 - j
-                    at = ((shift % 2) * 6 + t * 2 + p) * HALF + shift // 2
-                    grid = grid + col_taps[j] * mixed[at : at + wide, :]
-                grids.append(grid)
+            terms = [grids[e, 2 * t + p] for t in range(TERMS)]
             for a in range(TERMS):
-                value = inverse[a][0] * grids[0] + inverse[a][1] * grids[1] + inverse[a][2] * grids[2]
+                value = inverse[a][0] * terms[0] + inverse[a][1] * terms[1] + inverse[a][2] * terms[2]
                 out_ref[pl.ds(e * 6 + a * 2 + p, wide, stride=12), :] = value
-
-    for copy in row_copies:
-        copy.wait_send()
-    for chip in chips:
-
-        @pl.when(chip != me)
-        def _(chip=chip):
-            tile_to(chip).wait_send()
 
 
 def grid_round(chans, n_rows, width, which, arrays):
@@ -331,15 +352,20 @@
             pltpu.VMEM((n_vis // 128 * chans, 128), BF16),
             pltpu.VMEM((12 * HALF, 2 * ROWS_DEV), F32),
             pltpu.VMEM((12 * HALF, ROWS_DEV), F32),
-            pltpu.VMEM((8, 128), F32),
-            pltpu.VMEM((n_rows, 8, 128), F32),
+            pltpu.VMEM((2, 2 * TERMS, width // 2, ROWS_DEV), F32),
+            pltpu.VMEM((1, 128), F32),
+            pltpu.VMEM((chans, 1, 128), F32),
+            pltpu.VMEM((1, 128), F32),
+            pltpu.VMEM((n_rows, 1, 128), F32),
             pltpu.SemaphoreType.DMA((7,)),
             pltpu.SemaphoreType.REGULAR,
             pltpu.SemaphoreType.REGULAR,
-            pltpu.SemaphoreType.DMA((chans,)),
+            pltpu.SemaphoreType.DMA,
             pltpu.SemaphoreType.DMA((chans,)),
             pltpu.SemaphoreType.DMA((n_rows,)),
             pltpu.SemaphoreType.DMA((n_rows,)),
+            pltpu.SemaphoreType.DMA,
+            pltpu.SemaphoreType.DMA,
         ],
         compiler_params=pltpu.CompilerParams(
             collective_id=0, has_side_effects=True, vmem_limit_bytes=40 * 1024 * 1024

time: 20.5 us -> 19.4 us (0.946)
  Pallas kernels: 19.4 us -> 18.5 us
    pallas_call x1, Pallas kernels: 19.4 us -> 18.5 us  [grid_round(): pl.pallas_call(functools.partial(kernel, chans, n_rows, width), out_shape...]
where the time goes in v4:
time: 19.4 us; the launch traced here: 19.2 us
  Pallas kernels  18.5 us (95%)
  local copies, waits for them, and re-layouts  0.68 us (4%)
    pallas_call x1, Pallas kernels, grid_round(): pl.pallas_call(functools.partial(kernel, chans, n_rows, width), out_shape...  18.5 us
    unnamed x1, local copies, waits for them, and re-layouts  0.68 us

profile of v4, /device:TPU:1, one launch (start us, length us, event | category | flops | bytes accessed | tf_op | source)
XLA Modules:
  0.0 19.2 jit_solution(13006987696179332367)
XLA Ops:
  0.0 18.5 %shard_map.64 = (f32[384,128]{1,0:T(8,128)S(1)}, s32[1]{0:T(128)S(4)}) custom-call(s32[1]{0:T(128)} %constant.2.clone.1.round_hbm, s32[8,256]{1,0:T(8,128)} %row_hbm.1, s32[8,256]{1,0:T(8,128)} %col_hbm.1, f32[8,2,256]{2,1,0:T(2,128)} %vis_hbm.1, f32[8,256]{1,0:T(8,128)} %weight_hbm.1, f32[3,8]{1,0:T(4,128)} %bitcast.10, f32[8]{0:T(128)} %taps_hbm.1), custom_call_target="tpu_custom_call" | custom-call | tf_op jit(solution)/shard_map/pallas_call | solution.py:339
  18.6 0.7 %copy.17 = f32[64,3,2,128]{3,2,1,0:T(2,128)} copy(f32[64,3,2,128]{3,2,1,0:T(2,128)S(1)} %bitcast.9) | data formatting | bytes 393216
  (1 shorter events, 0.0 us)

commit v5 on v4

--- a/solution.py
+++ b/solution.py
@@ -15,7 +15,8 @@
 SLOTS = 128
 PAIRS = ((0, 0), (0, 1), (0, 2), (1, 1), (1, 2), (2, 2))
 ACROSS_X, ACROSS_Z = 4, 8
-Z_ORDER = (0, 1, 2, 3, 7, 6, 5, 4)
+Z_ORDER = (0, 1, 2, 3, 5, 6, 4, 7)
+LEAD = 1
 EARLY = 3
 HALF = 48
 PER_STEP = 4
@@ -52,8 +53,8 @@
     round_hbm, row_hbm, col_hbm, vis_hbm, weight_hbm, taylor_hbm, taps_hbm,
     out_ref, rounds_ref,
     round_ref, row_ref, col_ref, vis_ref, weight_ref, taylor_ref, taps_ref,
-    mine, theirs, a_ref, b_ref, e_ref, cells, mixed, grids, hess_mine, hess_chan, hess_sum, hess_rows,
-    in_sem, early_here, late_here, send_sem, recv_sem, row_send, row_recv, hess_send, hess_recv,
+    mine, theirs, a_ref, b_ref, e_ref, cells, mixed, grids, hess_mine, hess_chan, hess_sum, hess_rows, hess_lead,
+    in_sem, early_here, late_here, send_sem, recv_sem, row_send, row_recv, hess_send, hess_recv, lead_send, lead_recv,
 ):
     me, slab = lax.axis_index("chan"), lax.axis_index("rows")
     my_y, core = slab // 2, slab % 2
@@ -79,6 +80,9 @@
     n_late = 2 * chans - others - 2 + 2 * is_early.astype(jnp.int32) + n_rows - 1
     barrier = pltpu.get_barrier_semaphore()
     counter = 2 * my_y + 1 - is_early.astype(jnp.int32)
+    is_lead = (me == 0) & (slab == LEAD)
+    lead_told = my_y != LEAD // 2
+    n_early = n_early + lead_told.astype(jnp.int32)
     for chip in chips[::-1]:
 
         @pl.when(chip != me)
@@ -89,6 +93,15 @@
         there = (my_y + i) % (n_rows // 2)
         pl.semaphore_signal(barrier, inc=1, device_id=(me, 2 * there + 1), device_id_type=MESH)
     pl.semaphore_signal(barrier, inc=1, device_id=(me, slab + 1 - 2 * core), device_id_type=MESH)
+
+    @pl.when(is_lead)
+    def _():
+        for i in range(1, n_rows // 2):
+            there = (my_y + i) % (n_rows // 2)
+
+            @pl.loop(0, chans)
+            def _(k, there=there):
+                pl.semaphore_signal(barrier, inc=1, device_id=(chans - 1 - k, 2 * there), device_id_type=MESH)
 
     inputs[0].wait()
     inputs[1].wait()
@@ -158,6 +171,15 @@
     def _():
         pl.semaphore_wait(early_here, 1)
 
+    part_to_lead = pltpu.make_async_remote_copy(
+        src_ref=hess_mine, dst_ref=hess_lead.at[slab, me], send_sem=lead_send, recv_sem=lead_recv,
+        device_id=(0, LEAD), device_id_type=MESH,
+    )
+
+    @pl.when(slab != LEAD)
+    def _():
+        part_to_lead.start()
+
     to_chips(True, lambda chip: part_with(chip, me).start())
 
     start = jnp.zeros((2 * half, 128), F32)
@@ -269,14 +291,20 @@
     chan_sum = gather(hess_chan[...])
     hess_sum[...] = chan_sum
     hess_rows[pl.ds(slab, 1)] = chan_sum[None]
-    row_copies = []
-    for i in range(1, n_rows):
-        copy = pltpu.make_async_remote_copy(
+    def row_copy(i):
+        return pltpu.make_async_remote_copy(
             src_ref=hess_sum, dst_ref=hess_rows.at[slab], send_sem=row_send.at[i], recv_sem=row_recv.at[i],
             device_id=(me, (slab + i) % n_rows), device_id_type=MESH,
         )
-        copy.start()
-        row_copies.append(copy)
+
+    def to_row(use):
+        for i in range(1, n_rows):
+
+            @pl.when((me != 0) | ((slab + i) % n_rows != LEAD))
+            def _(i=i):
+                use(row_copy(i))
+
+    to_row(lambda copy: copy.start())
 
     for g in range(0, chans, PER_STEP):
         arrived(g)
@@ -306,9 +334,28 @@
         send_sem=send_sem, recv_sem=recv_sem.at[0], device_id=(me, slab), device_id_type=MESH,
     ).wait_send()
 
-    for copy in row_copies:
-        copy.wait()
-    hess = gather(hess_rows[...])
+    to_row(lambda copy: copy.wait_send())
+
+    @pl.when(slab != LEAD)
+    def _():
+        part_to_lead.wait_send()
+
+    @pl.when(is_lead)
+    def _():
+        pltpu.make_async_remote_copy(
+            src_ref=hess_lead.at[pl.ds(0, n_rows - 1)], dst_ref=hess_lead.at[pl.ds(0, n_rows - 1)],
+            send_sem=lead_send, recv_sem=lead_recv, device_id=(me, slab), device_id_type=MESH,
+        ).wait_recv()
+        total = [gather(hess_lead[r]) for r in range(n_rows) if r != LEAD] + [hess_sum[...]]
+        hess_mine[...] = gather(jnp.stack(total))
+
+    @pl.when(jnp.logical_not(is_lead))
+    def _():
+        for i in range(1, n_rows):
+            row_copy(i).wait_recv()
+        hess_mine[...] = gather(hess_rows[...])
+
+    hess = hess_mine[...]
     entries = {}
     for i, (a, b) in enumerate(PAIRS):
         entries[a, b] = entries[b, a] = jnp.sum(jnp.where(lane == i, hess, 0.0), axis=1, keepdims=True)
@@ -357,6 +404,7 @@
             pltpu.VMEM((chans, 1, 128), F32),
             pltpu.VMEM((1, 128), F32),
             pltpu.VMEM((n_rows, 1, 128), F32),
+            pltpu.VMEM((n_rows, chans, 1, 128), F32),
             pltpu.SemaphoreType.DMA((7,)),
             pltpu.SemaphoreType.REGULAR,
             pltpu.SemaphoreType.REGULAR,
@@ -364,6 +412,8 @@
             pltpu.SemaphoreType.DMA((chans,)),
             pltpu.SemaphoreType.DMA((n_rows,)),
             pltpu.SemaphoreType.DMA((n_rows,)),
+            pltpu.SemaphoreType.DMA,
+            pltpu.SemaphoreType.DMA,
             pltpu.SemaphoreType.DMA,
             pltpu.SemaphoreType.DMA,
         ],

time: 19.4 us -> 18.5 us (0.954)
  the two profiles are of different devices: /device:TPU:1 before, /device:TPU:160 now
where the time goes in v5:
time: 18.5 us; the launch traced here: 18.4 us
  Pallas kernels  17.7 us (96%)
  local copies, waits for them, and re-layouts  0.68 us (4%)
    pallas_call x1, Pallas kernels, grid_round(): pl.pallas_call(functools.partial(kernel, chans, n_rows, width), out_shape...  17.7 us
    unnamed x1, local copies, waits for them, and re-layouts  0.68 us

profile of v5, /device:TPU:160, one launch (start us, length us, event | category | flops | bytes accessed | tf_op | source)
XLA Modules:
  0.0 18.4 jit_solution(7611399323004991191)
XLA Ops:
  0.0 17.7 %shard_map.64 = (f32[384,128]{1,0:T(8,128)S(1)}, s32[1]{0:T(128)S(4)}) custom-call(s32[1]{0:T(128)} %constant.2.clone.1.round_hbm, s32[8,256]{1,0:T(8,128)} %row_hbm.1, s32[8,256]{1,0:T(8,128)} %col_hbm.1, f32[8,2,256]{2,1,0:T(2,128)} %vis_hbm.1, f32[8,256]{1,0:T(8,128)} %weight_hbm.1, f32[3,8]{1,0:T(4,128)} %bitcast.10, f32[8]{0:T(128)} %taps_hbm.1), custom_call_target="tpu_custom_call" | custom-call | tf_op jit(solution)/shard_map/pallas_call | solution.py:386
  17.7 0.7 %copy.17 = f32[64,3,2,128]{3,2,1,0:T(2,128)} copy(f32[64,3,2,128]{3,2,1,0:T(2,128)S(1)} %bitcast.9) | data formatting | bytes 393216
  (1 shorter events, 0.0 us)

commit v6 on v5

--- a/solution.py
+++ b/solution.py
@@ -15,10 +15,10 @@
 SLOTS = 128
 PAIRS = ((0, 0), (0, 1), (0, 2), (1, 1), (1, 2), (2, 2))
 ACROSS_X, ACROSS_Z = 4, 8
-Z_ORDER = (0, 1, 2, 3, 5, 6, 4, 7)
+Z_ORDER = (0, 1, 2, 5, 6, 7, 3, 4)
 LEAD = 1
 EARLY = 3
-HALF = 48
+HALF = 40
 PER_STEP = 4
 
 MESH = pl.DeviceIdType.MESH
@@ -28,7 +28,8 @@
 
 
 def in_order_of_start():
-    return [x * ACROSS_Z + z for z in Z_ORDER for x in range(ACROSS_X)]
+    early = [x * ACROSS_Z + z for z in Z_ORDER[:EARLY] for x in range(ACROSS_X)]
+    return early + [x * ACROSS_Z + z for x in range(ACROSS_X) for z in Z_ORDER[EARLY:]]
 
 
 def matmul_nt(a, b):
@@ -83,7 +84,7 @@
     is_lead = (me == 0) & (slab == LEAD)
     lead_told = my_y != LEAD // 2
     n_early = n_early + lead_told.astype(jnp.int32)
-    for chip in chips[::-1]:
+    for chip in chips:
 
         @pl.when(chip != me)
         def _(chip=chip):
@@ -254,6 +255,7 @@
     for k in range(SUPPORT):
         row_taps = jnp.where(tap_of == k, taps_ref[k], row_taps)
     row_high, row_low = two_parts(row_taps)
+    twice_high = jnp.concatenate([row_high, row_high], axis=0)
 
     half_cell = iota((HALF, 128), 0).astype(F32)
     row_cell = iota((2 * ROWS_DEV, 128), 0).astype(F32)
@@ -277,9 +279,9 @@
             here = half_cell == halves
             a_parts.append(
                 jnp.concatenate(
-                    [jnp.where(here, part_of[v : v + 1], 0.0).astype(BF16) for part_of in (high, low) for v in range(6)],
+                    [jnp.where(here, part_of[v : v + 1], 0.0) for part_of in (high, low) for v in range(6)],
                     axis=0,
-                )
+                ).astype(BF16)
             )
         total = matmul_nt(jnp.concatenate(a_parts, axis=1), jnp.concatenate(b_parts, axis=1))
         if g == 0:
@@ -314,7 +316,7 @@
         x = cells[: 6 * HALF, par * 128 : par * 128 + 128] + cells[6 * HALF :, par * 128 : par * 128 + 128]
         high, low = two_parts(x)
         mixed[par * 6 * HALF : (par + 1) * 6 * HALF, :] = (
-            matmul(high, row_high) + matmul(low, row_high) + matmul(high, row_low)
+            matmul(jnp.concatenate([high, low], axis=1), twice_high) + matmul(high, row_low)
         )
 
     wide = width // 2

time: 18.5 us -> 18.1 us (0.978)
  the two profiles are of different devices: /device:TPU:160 before, /device:TPU:1 now
where the time goes in v6:
time: 18.1 us; the launch traced here: 17.7 us
  Pallas kernels  17 us (94%)
  local copies, waits for them, and re-layouts  0.68 us (4%)
    pallas_call x1, Pallas kernels, grid_round(): pl.pallas_call(functools.partial(kernel, chans, n_rows, width), out_shape...  17 us
    unnamed x1, local copies, waits for them, and re-layouts  0.68 us

profile of v6, /device:TPU:1, one launch (start us, length us, event | category | flops | bytes accessed | tf_op | source)
XLA Modules:
  0.0 17.7 jit_solution(12526897649237416682)
XLA Ops:
  0.0 17.0 %shard_map.64 = (f32[384,128]{1,0:T(8,128)S(1)}, s32[1]{0:T(128)S(4)}) custom-call(s32[1]{0:T(128)} %constant.2.clone.1.round_hbm, s32[8,256]{1,0:T(8,128)} %row_hbm.1, s32[8,256]{1,0:T(8,128)} %col_hbm.1, f32[8,2,256]{2,1,0:T(2,128)} %vis_hbm.1, f32[8,256]{1,0:T(8,128)} %weight_hbm.1, f32[3,8]{1,0:T(4,128)} %bitcast.10, f32[8]{0:T(128)} %taps_hbm.1), custom_call_target="tpu_custom_call" | custom-call | tf_op jit(solution)/shard_map/pallas_call | solution.py:388
  17.1 0.7 %copy.17 = f32[64,3,2,128]{3,2,1,0:T(2,128)} copy(f32[64,3,2,128]{3,2,1,0:T(2,128)S(1)} %bitcast.9) | data formatting | bytes 393216
  (1 shorter events, 0.0 us)

commit v7 on v6

--- a/solution.py
+++ b/solution.py
@@ -293,18 +293,18 @@
     chan_sum = gather(hess_chan[...])
     hess_sum[...] = chan_sum
     hess_rows[pl.ds(slab, 1)] = chan_sum[None]
-    def row_copy(i):
+    def row_copy(to, sender):
         return pltpu.make_async_remote_copy(
-            src_ref=hess_sum, dst_ref=hess_rows.at[slab], send_sem=row_send.at[i], recv_sem=row_recv.at[i],
-            device_id=(me, (slab + i) % n_rows), device_id_type=MESH,
+            src_ref=hess_sum, dst_ref=hess_rows.at[sender], send_sem=row_send.at[to], recv_sem=row_recv.at[sender],
+            device_id=(me, to), device_id_type=MESH,
         )
 
     def to_row(use):
-        for i in range(1, n_rows):
-
-            @pl.when((me != 0) | ((slab + i) % n_rows != LEAD))
-            def _(i=i):
-                use(row_copy(i))
+        for to in range(n_rows):
+
+            @pl.when((slab != to) & (me != 0) if to == LEAD else slab != to)
+            def _(to=to):
+                use(row_copy(to, slab))
 
     to_row(lambda copy: copy.start())
 
@@ -353,8 +353,12 @@
 
     @pl.when(jnp.logical_not(is_lead))
     def _():
-        for i in range(1, n_rows):
-            row_copy(i).wait_recv()
+        for sender in range(n_rows):
+
+            @pl.when(sender != slab)
+            def _(sender=sender):
+                row_copy(sender, sender).wait_recv()
+
         hess_mine[...] = gather(hess_rows[...])
 
     hess = hess_mine[...]

time: 18.1 us -> 18 us (level)
  no operation moved by 1% of the time
where the time goes in v7:
time: 18 us; the launch traced here: 17.7 us
  Pallas kernels  17 us (94%)
  local copies, waits for them, and re-layouts  0.68 us (4%)
    pallas_call x1, Pallas kernels, grid_round(): pl.pallas_call(functools.partial(kernel, chans, n_rows, width), out_shape...  17 us
    unnamed x1, local copies, waits for them, and re-layouts  0.68 us

profile of v7, /device:TPU:1, one launch (start us, length us, event | category | flops | bytes accessed | tf_op | source)
XLA Modules:
  0.0 17.7 jit_solution(15953851670811913014)
XLA Ops:
  0.0 17.0 %shard_map.64 = (f32[384,128]{1,0:T(8,128)S(1)}, s32[1]{0:T(128)S(4)}) custom-call(s32[1]{0:T(128)} %constant.2.clone.1.round_hbm, s32[8,256]{1,0:T(8,128)} %row_hbm.1, s32[8,256]{1,0:T(8,128)} %col_hbm.1, f32[8,2,256]{2,1,0:T(2,128)} %vis_hbm.1, f32[8,256]{1,0:T(8,128)} %weight_hbm.1, f32[3,8]{1,0:T(4,128)} %bitcast.10, f32[8]{0:T(128)} %taps_hbm.1), custom_call_target="tpu_custom_call" | custom-call | tf_op jit(solution)/shard_map/pallas_call | solution.py:392
  17.1 0.7 %copy.17 = f32[64,3,2,128]{3,2,1,0:T(2,128)} copy(f32[64,3,2,128]{3,2,1,0:T(2,128)S(1)} %bitcast.9) | data formatting | bytes 393216
  (1 shorter events, 0.0 us)
